TPU v7x, 512 devices: a whole 4x4x16 slice. The times are simulated.
512 devices in a mesh: tm: 32 (over y, x, core), head: 16 (over z).
Axes of the slice: x: 4, y: 4, z: 16, core: 2. Of those that a mesh axis runs over, the one named last changes fastest.
Arguments:
- frame_inputs: bfloat16 [32768, 4096], P('tm', 'head'), may hold values from -6 to 6
- write_map: bfloat16 [32768, 128], P('tm'), may hold values from -0.29882812 to 0.29882812
- read_map: bfloat16 [32768, 128], P('tm'), may hold values from -0.29882812 to 0.29882812
- log_decay: float32 [64, 32768], P('head', 'tm'), may hold values from -1 to 0, as said below
- out_weight: bfloat16 [2048, 4096], P(None, 'head'), may hold values from -0.09375 to 0.09375
- caption_grad: float32 [1024, 2048], P('tm', 'head'), may hold values from -150 to 150
- caption_start: int32 [1024], P('tm'), may hold values from 0 to 32767, as said below
- caption_end: int32 [1024], P('tm'), may hold values from 1 to 32768, as said below
Outputs:
- grad_inputs: bfloat16 [32768, 4096], P('tm', 'head')
- grad_write: float32 [32768, 128], P(('tm', 'head'))
- grad_read: float32 [32768, 128], P(('tm', 'head'))
- grad_out_weight: float32 [2048, 4096], P('tm', 'head')
Inputs may be any that keep to these rules, and one draw needn't show every extreme that they name: `caption_start`: caption k belongs to index k // 32 of tm: its segment starts in that index's frames, at 1024 * (k // 32) or later and before 1024 * (k // 32 + 1). `caption_end`: each segment has at most 200 frames and at least one; some caption's segment has exactly 200. Segments of different captions may share frames, and a segment may end in the following index's frames. `log_decay`: every entry is negative.
All inputs are finite; a program needn't handle non-finite values.
Results may differ from a plain program's by a relative error of at most 0.022.
Values may be sent and summed in bfloat16 or wider, within the bound.
A program may use at most 64 MiB of HBM per device.

v0:
```python
import jax
import jax.numpy as jnp
from jax import lax
from jax.sharding import PartitionSpec as P

BLOCK = 256


HIGH = lax.Precision.HIGHEST


def from_behind(shard, axis, by):
    peers = lax.axis_size(axis)
    pairs = [(i, i + by) for i in range(peers) if 0 <= i + by < peers]
    return lax.ppermute(shard, axis, pairs)


def segment_weights(frame_ids, starts, ends):
    seg_len = jnp.maximum(ends - starts, 1.0)
    inside = (frame_ids[:, None] >= starts[None, :]) & (frame_ids[:, None] < ends[None, :])
    return jnp.where(inside, 1.0 / seg_len[None, :], 0.0)


def pool_back(frame_ids, own_rows, own_start, own_end, prev_rows, prev_start, prev_end):
    caption_rows = jnp.concatenate([prev_rows, own_rows], axis=0)
    weights = segment_weights(
        frame_ids, jnp.concatenate([prev_start, own_start]), jnp.concatenate([prev_end, own_end])
    )
    return jnp.dot(weights, caption_rows, precision=HIGH).astype(jnp.bfloat16)


def body(
    frame_inputs,
    write_map,
    read_map,
    log_decay,
    out_weight,
    caption_grad,
    caption_start,
    caption_end,
):
    frames = frame_inputs.shape[0]
    head_count = log_decay.shape[0]
    head_size = frame_inputs.shape[1] // head_count
    state_dim = write_map.shape[1]
    block_count = frames // BLOCK
    tm_index = lax.axis_index("tm")
    frame_ids = (tm_index * frames + jnp.arange(frames)).astype(jnp.float32)
    inputs = frame_inputs.reshape(block_count, BLOCK, head_count, head_size)
    write_rows = write_map.reshape(block_count, BLOCK, state_dim)
    read_rows = read_map.reshape(block_count, BLOCK, state_dim)
    running = jnp.swapaxes(
        jnp.cumsum(log_decay.reshape(head_count, block_count, BLOCK), axis=2), 0, 1
    )
    totals = running[:, :, -1]
    causal = jnp.arange(BLOCK)[:, None] >= jnp.arange(BLOCK)[None, :]
    log_gap = running[:, :, :, None] - running[:, :, None, :]
    decay_mat = jnp.where(causal, jnp.exp(jnp.where(causal, log_gap, 0.0)), 0.0)
    intersection = jnp.einsum(
        "ctn,csn->cts", read_rows, write_rows, preferred_element_type=jnp.float32
    )
    scores = (intersection[:, None] * decay_mat).astype(jnp.bfloat16)
    growth = jnp.exp(running)
    fading = jnp.exp(totals[:, :, None] - running)
    weighted_write = (fading[..., None] * write_rows[:, None]).astype(jnp.bfloat16)
    block_states = jnp.einsum(
        "chsn,cshp->chnp", weighted_write, inputs, preferred_element_type=jnp.float32
    )
    dev_log = jnp.sum(totals, axis=0)
    dev_state = jnp.zeros_like(block_states[0])
    for block in range(block_count):
        dev_state = jnp.exp(totals[block])[:, None, None] * dev_state + block_states[block]
    own_start = caption_start.astype(jnp.float32)
    own_end = caption_end.astype(jnp.float32)
    prev_rows, prev_start, prev_end = from_behind((caption_grad, own_start, own_end), "tm", 1)
    local_grad = pool_back(
        frame_ids, caption_grad, own_start, own_end, prev_rows, prev_start, prev_end
    )
    frame_grad = lax.all_gather(local_grad, "head", axis=1, tiled=True)
    grad_y = jnp.dot(frame_grad, out_weight, preferred_element_type=jnp.float32).astype(
        jnp.bfloat16
    )
    grads = grad_y.reshape(block_count, BLOCK, head_count, head_size)
    pairing = jnp.einsum("cthp,cshp->chts", inputs, grads, preferred_element_type=jnp.float32)
    cross_terms = (decay_mat * jnp.swapaxes(pairing, 2, 3)).astype(jnp.bfloat16)
    weighted_read = (growth[..., None] * read_rows[:, None]).astype(jnp.bfloat16)
    block_adjoint = jnp.einsum(
        "chsn,cshp->chnp", weighted_read, grads, preferred_element_type=jnp.float32
    )
    dev_adjoint = jnp.zeros_like(block_adjoint[0])
    for block in range(block_count - 1, -1, -1):
        dev_adjoint = jnp.exp(totals[block])[:, None, None] * dev_adjoint + block_adjoint[block]
    logs_all, states_all, adjoint_all = (
        lax.all_gather(dev_log[None], "tm", axis=0, tiled=True),
        lax.all_gather(dev_state[None], "tm", axis=0, tiled=True),
        lax.all_gather(dev_adjoint[None], "tm", axis=0, tiled=True),
    )
    inclusive = jnp.cumsum(logs_all, axis=0)
    before = inclusive - logs_all
    own_total = lax.dynamic_index_in_dim(inclusive, tm_index, 0, keepdims=False)
    own_before = lax.dynamic_index_in_dim(before, tm_index, 0, keepdims=False)
    rank_ids = jnp.arange(logs_all.shape[0])[:, None]
    ahead_log = jnp.where(rank_ids < tm_index, own_before[None] - inclusive, 0.0)
    state_w = jnp.where(rank_ids < tm_index, jnp.exp(ahead_log), 0.0)
    behind = jnp.where(rank_ids > tm_index, before - own_total[None], 0.0)
    adjoint_w = jnp.where(rank_ids > tm_index, jnp.exp(behind), 0.0)
    state_head = jnp.einsum("jh,jhnp->hnp", state_w, states_all, precision=HIGH)
    adjoint_tail = jnp.einsum("jh,jhnp->hnp", adjoint_w, adjoint_all, precision=HIGH)
    entry_states = []
    carry_state = state_head
    for block in range(block_count):
        entry_states.append(carry_state)
        carry_state = jnp.exp(totals[block])[:, None, None] * carry_state + block_states[block]
    entry_b = jnp.stack(entry_states).astype(jnp.bfloat16)
    exit_states = [carry_state] * block_count
    carry_adj = adjoint_tail
    for block in range(block_count - 1, -1, -1):
        exit_states[block] = carry_adj
        carry_adj = jnp.exp(totals[block])[:, None, None] * carry_adj + block_adjoint[block]
    exit_b = jnp.stack(exit_states).astype(jnp.bfloat16)
    growth_t = jnp.swapaxes(growth, 1, 2)[..., None]
    fading_t = jnp.swapaxes(fading, 1, 2)[..., None]
    out_intra = jnp.einsum("chts,cshp->cthp", scores, inputs, preferred_element_type=jnp.float32)
    out_inter = (
        jnp.einsum("ctn,chnp->cthp", read_rows, entry_b, preferred_element_type=jnp.float32)
        * growth_t
    )
    layer_out = (out_intra + out_inter).astype(jnp.bfloat16).reshape(frames, head_count * head_size)
    in_intra = jnp.einsum("chst,cshp->cthp", scores, grads, preferred_element_type=jnp.float32)
    in_inter = (
        jnp.einsum("ctn,chnp->cthp", write_rows, exit_b, preferred_element_type=jnp.float32)
        * fading_t
    )
    grad_inputs = (in_intra + in_inter).astype(jnp.bfloat16).reshape(frames, head_count * head_size)
    read_intra = jnp.einsum(
        "chts,csn->ctn", cross_terms, write_rows, preferred_element_type=jnp.float32
    )
    read_inter = jnp.sum(
        jnp.einsum("chnp,cthp->chtn", entry_b, grads, preferred_element_type=jnp.float32)
        * growth[..., None],
        axis=1,
    )
    write_intra = jnp.einsum(
        "chst,csn->ctn", cross_terms, read_rows, preferred_element_type=jnp.float32
    )
    write_inter = jnp.sum(
        jnp.einsum("chnp,cthp->chtn", exit_b, inputs, preferred_element_type=jnp.float32)
        * fading[..., None],
        axis=1,
    )
    grad_read_part = (read_intra + read_inter).reshape(frames, state_dim)
    grad_write_part = (write_intra + write_inter).reshape(frames, state_dim)
    grad_out_weight = lax.psum_scatter(
        lax.dot_general(
            frame_grad, layer_out, (((0,), (0,)), ((), ())), preferred_element_type=jnp.float32
        ).astype(jnp.bfloat16),
        "tm",
        scatter_dimension=0,
        tiled=True,
    ).astype(jnp.float32)
    grad_write, grad_read = (
        lax.psum_scatter(
            grad_write_part.astype(jnp.bfloat16), "head", scatter_dimension=0, tiled=True
        ).astype(jnp.float32),
        lax.psum_scatter(
            grad_read_part.astype(jnp.bfloat16), "head", scatter_dimension=0, tiled=True
        ).astype(jnp.float32),
    )
    return (grad_inputs, grad_write, grad_read, grad_out_weight)


def solution(mesh):
    in_specs = (
        P("tm", "head"),
        P("tm", None),
        P("tm", None),
        P("head", "tm"),
        P(None, "head"),
        P("tm", "head"),
        P("tm"),
        P("tm"),
    )
    out_specs = (P("tm", "head"), P(("tm", "head"), None), P(("tm", "head"), None), P("tm", "head"))
    return jax.shard_map(body, mesh=mesh, in_specs=in_specs, out_specs=out_specs, check_vma=False)
```

profile of v0, /device:TPU:24, one launch (start us, length us, event | category | flops | bytes accessed | tf_op | source)
XLA Modules:
  0.0 507.9 jit_solution(1235885712006712893)
XLA Ops:
  8.0 1.9 collective-permute-start
  10.6 3.5 collective-permute-start.1
  14.1 1.9 collective-permute-start.2
  17.6 3.8 collective-permute-done.2
  21.5 2.1 convolution_convert_fusion.2
  24.3 4.8 reduce-window.6
  31.5 2.0 reshape.167
  35.7 85.6 %all-gather.5.cloned.1.call-done = bf16[1024,2048]{1,0:T(8,128)(2,1)} async-done(((bf16[1024,128]{1,0:T(8,128)(2,1)}), bf16[1024,2048]{1,0:T(8,128)(2,1)}) %all-gather.5.cloned.1.call-update) | async-done | bytes 4194320 | tf_op jit(solution)/shard_map/all_gather | solution.py:79
  121.3 4.2 convolution_convert_fusion.1
  125.6 2.1 reshape.166
  128.9 2.0 fusion.12
  134.8 53.4 %all-reduce = f32[128]{0:T(128)S(1)} all-reduce(f32[128]{0:T(128)S(1)} %dynamic-update-slice), channel_id=2, replica_groups=mesh['tm'=32,'head'=16] {'tm'}, use_global_device_ids=true, to_apply=%add | all-reduce | flops 128 | bytes 1024
  189.9 3.5 fusion.3
  193.5 2.5 convert_reduce_fusion
  196.0 2.5 multiply_reduce_fusion.1
  198.5 53.5 %all-gather.9.cloned.1.call-done = f32[32,4,128,64]{2,3,1,0:T(8,128)} async-done(((f32[1,4,128,64]{2,3,1,0:T(8,128)}), f32[32,4,128,64]{2,3,1,0:T(8,128)}) %all-gather.9.cloned.1.call-update) | async-done | bytes 4194320 | tf_op jit(solution)/shard_map/all_gather | solution.py:95
  252.1 2.6 multiply_reduce_fusion
  260.5 2.1 multiply_reduce_fusion.3
  263.8 2.1 fusion.10
  268.8 2.3 convolution_convert_fusion
  271.2 2.5 fusion.2
  276.1 51.8 %reduce-scatter.6.cloned.1.call-done = bf16[64,128]{1,0:T(8,128)(2,1)} async-done(((bf16[1024,128]{1,0:T(8,128)(2,1)}), bf16[64,128]{1,0:T(8,128)(2,1)}) %reduce-scatter.6.cloned.1.call-update) | async-done | bytes 16400 | tf_op jit(solution)/shard_map/reduce_scatter | solution.py:165
  329.3 68.1 %reduce-scatter.4.cloned.1.call-done = bf16[64,128]{1,0:T(8,128)(2,1)} async-done(((bf16[1024,128]{1,0:T(8,128)(2,1)}), bf16[64,128]{1,0:T(8,128)(2,1)}) %reduce-scatter.4.cloned.1.call-update) | async-done | bytes 16400 | tf_op jit(solution)/shard_map/reduce_scatter | solution.py:162
  398.7 101.0 %reduce-scatter.8.cloned.1.call-done = bf16[64,256]{1,0:T(8,128)(2,1)} async-done(((bf16[2048,256]{1,0:T(8,128)(2,1)}), bf16[64,256]{1,0:T(8,128)(2,1)}) %reduce-scatter.8.cloned.1.call-update) | async-done | bytes 32784 | tf_op jit(solution)/shard_map/reduce_scatter | solution.py:153
  (124 shorter events, 30.6 us)
Async XLA Ops:
  7.2 114.2 %copy-start = (bf16[2048,256]{1,0:T(8,128)(2,1)S(1)}, bf16[2048,256]{1,0:T(8,128)(2,1)}, u32[]{:S(2)}) copy-start(bf16[2048,256]{1,0:T(8,128)(2,1)} %param.12) | copy-start | bytes 3145732
  7.2 26.9 %copy-start.2 = (bf16[1024,128]{1,0:T(8,128)(2,1)S(1)}, bf16[1024,128]{1,0:T(8,128)(2,1)}, u32[]{:S(2)}) copy-start(bf16[1024,128]{1,0:T(8,128)(2,1)} %param.9) | copy-start | bytes 786436
  7.2 114.1 %all-gather.5.cloned.1.call-start = ((), (), s32[]{:S(2)}) async-start(), calls=%async_computation.3 | async-start | bytes 4456448 | tf_op jit(solution)/shard_map/all_gather | solution.py:79
  8.0 8.0 %collective-permute-start = (f32[32]{0:T(128)S(1)}, f32[32]{0:T(128)S(1)}, u32[]{:S(2)}, u32[]{:S(2)}) collective-permute-start(f32[32]{0:T(128)S(1)} %convert_element_type.84), channel_id=1, source_target_pairs={{0,16},{16,32},{32,48},{48,64},{64,80},{80,96},{96,112},{112,128},... | collective-permute-start | bytes 392 | tf_op jit(solution)/shard_map/ppermute | solution.py:15
  10.6 7.0 %collective-permute-start.1 = (f32[32]{0:T(128)S(1)}, f32[32]{0:T(128)S(1)}, u32[]{:S(2)}, u32[]{:S(2)}) collective-permute-start(f32[32]{0:T(128)S(1)} %convert_element_type.85), channel_id=1, source_target_pairs={{0,16},{16,32},{32,48},{48,64},{64,80},{80,96},{96,112},{112,128},... | collective-permute-start | bytes 392 | tf_op jit(solution)/shard_map/ppermute | solution.py:15
  14.1 7.4 %collective-permute-start.2 = (f32[32,128]{1,0:T(8,128)}, f32[32,128]{1,0:T(8,128)S(1)}, u32[]{:S(2)}, u32[]{:S(2)}) collective-permute-start(f32[32,128]{1,0:T(8,128)} %param.13), channel_id=1, source_target_pairs={{0,16},{16,32},{32,48},{48,64},{64,80},{80,96},{96,112},{112,128},... | collective-permute-start | bytes 49160 | tf_op jit(solution)/shard_map/ppermute | solution.py:15
  23.5 172.4 %all-gather.7.cloned.1.call-start = ((), (), s32[]{:S(2)}) async-start(), calls=%async_computation.4 | async-start | bytes 4325376 | tf_op jit(solution)/shard_map/all_gather | solution.py:96
  29.7 163.8 %copy-start.21 = (f32[4,4,256]{2,0,1:T(4,128)}, f32[4,4,256]{2,0,1:T(4,128)S(1)}, u32[]{:S(2)}) copy-start(f32[4,4,256]{2,0,1:T(4,128)S(1)} %copy.143) | copy-start | bytes 49156
  34.0 87.3 %copy-start.4 = (bf16[4,256,4,64]{1,3,2,0:T(8,128)(2,1)}, bf16[4,256,4,64]{1,3,2,0:T(8,128)(2,1)S(1)}, u32[]{:S(2)}) copy-start(bf16[4,256,4,64]{1,3,2,0:T(8,128)(2,1)S(1)} %copy.104) | copy-start | bytes 1572868
  34.3 96.6 %copy-start.24 = (f32[4]{0:T(128)}, f32[4]{0:T(128)S(1)}, u32[]{:S(2)}) copy-start(f32[4]{0:T(128)S(1)} %get-tuple-element.24) | copy-start | bytes 52
  34.3 96.6 %copy-start.25 = (f32[4]{0:T(128)}, f32[4]{0:T(128)S(1)}, u32[]{:S(2)}) copy-start(f32[4]{0:T(128)S(1)} %get-tuple-element.22) | copy-start | bytes 52
  34.4 96.6 %copy-start.26 = (f32[4]{0:T(128)}, f32[4]{0:T(128)S(1)}, u32[]{:S(2)}) copy-start(f32[4]{0:T(128)S(1)} %get-tuple-element.23) | copy-start | bytes 52
  34.4 96.6 %copy-start.27 = (f32[4]{0:T(128)}, f32[4]{0:T(128)S(1)}, u32[]{:S(2)}) copy-start(f32[4]{0:T(128)S(1)} %get-tuple-element.25) | copy-start | bytes 52
  34.6 91.0 %copy-start.23 = (f32[4,4]{1,0:T(4,128)}, f32[4,4]{1,0:T(4,128)S(1)}, u32[]{:S(2)}) copy-start(f32[4,4]{1,0:T(4,128)S(1)} %get-tuple-element.21) | copy-start | bytes 196
  34.7 86.7 %copy-start.15 = (f32[4,4,256]{2,1,0:T(4,128)}, f32[4,4,256]{2,1,0:T(4,128)S(1)}, u32[]{:S(2)}) copy-start(f32[4,4,256]{2,1,0:T(4,128)S(1)} %get-tuple-element.41) | copy-start | bytes 49156
  34.7 94.2 %copy-start.16 = (f32[4,4,256]{2,1,0:T(4,128)}, f32[4,4,256]{2,1,0:T(4,128)S(1)}, u32[]{:S(2)}) copy-start(f32[4,4,256]{2,1,0:T(4,128)S(1)} %get-tuple-element.42) | copy-start | bytes 49156
  125.6 63.0 %copy-start.1 = (bf16[1024,128]{1,0:T(8,128)(2,1)S(1)}, bf16[1024,128]{1,0:T(8,128)(2,1)}, u32[]{:S(2)}) copy-start(bf16[1024,128]{1,0:T(8,128)(2,1)} %param.10) | copy-start | bytes 786436
  131.8 120.3 %all-gather.9.cloned.1.call-start = ((), (), s32[]{:S(2)}) async-start(), calls=%async_computation.6 | async-start | bytes 4325376 | tf_op jit(solution)/shard_map/all_gather | solution.py:95
  132.5 195.4 %reduce-scatter.6.cloned.1.call-start = ((), (), s32[]{:S(2)}) async-start(), calls=%async_computation.7 | async-start | bytes 278528 | tf_op jit(solution)/shard_map/reduce_scatter | solution.py:165
  252.1 6.0 %copy-start.7 = (bf16[4,256,256]{2,1,0:T(8,128)(2,1)S(1)}, bf16[4,256,256]{2,1,0:T(8,128)(2,1)}, u32[]{:S(2)}) copy-start(bf16[4,256,256]{2,1,0:T(8,128)(2,1)} %convert_reduce_fusion) | copy-start | bytes 1572868
  259.1 7.1 %copy-start.10 = (bf16[1,4,128,64]{2,3,1,0:T(8,128)(2,1)S(1)}, bf16[1,4,128,64]{2,3,1,0:T(8,128)(2,1)}, u32[]{:S(2)}) copy-start(bf16[1,4,128,64]{2,3,1,0:T(8,128)(2,1)} %copy-done.9) | copy-start | bytes 196612
  259.1 7.1 %copy-start.12 = (bf16[1,4,128,64]{2,3,1,0:T(8,128)(2,1)S(1)}, bf16[1,4,128,64]{2,3,1,0:T(8,128)(2,1)}, u32[]{:S(2)}) copy-start(bf16[1,4,128,64]{2,3,1,0:T(8,128)(2,1)} %copy-done.11) | copy-start | bytes 196612
  259.2 138.2 %reduce-scatter.4.cloned.1.call-start = ((), (), s32[]{:S(2)}) async-start(), calls=%async_computation.5 | async-start | bytes 278528 | tf_op jit(solution)/shard_map/reduce_scatter | solution.py:162
  265.9 233.7 %reduce-scatter.8.cloned.1.call-start = ((), (), s32[]{:S(2)}) async-start(), calls=%async_computation.8 | async-start | bytes 1081344 | tf_op jit(solution)/shard_map/reduce_scatter | solution.py:153
  (14 other events, 47.6 us)
Sparse Core Ops, SparseCore 0:
  23.7 97.6 all-gather.4
  131.9 56.0 all-gather.6
  191.2 60.8 all-gather.8
  259.3 68.5 reduce-scatter.5
  330.8 66.4 reduce-scatter.3
  401.6 98.0 reduce-scatter.7
where the time goes:
time: 509 us; the launch traced here: 508 us
  waiting for transfers between devices  366 us (72%)
  blocking collectives  53.4 us (10%)
  matrix products  29.5 us (6%)
  other arithmetic  21.7 us (4%)
  between operations  15.3 us (3%)
  local copies, waits for them, and re-layouts  14.1 us (3%)
  starting transfers between devices  7.75 us (2%)
    reduce_scatter x1, waiting for transfers between devices, body(): lax.psum_scatter(lax.dot_general(frame_grad, layer_out, (((0,), (0,)), ((...  101 us
    all_gather x1, waiting for transfers between devices, body(): frame_grad = lax.all_gather(local_grad, 'head', axis=1, tiled=True)  85.6 us
    reduce_scatter x1, waiting for transfers between devices, body(): lax.psum_scatter(grad_write_part.astype(jnp.bfloat16), 'head', scatter_di...  68.1 us
    all_gather x1, waiting for transfers between devices, body(): lax.all_gather(dev_state[None], 'tm', axis=0, tiled=True)  53.5 us
    unnamed x1, blocking collectives  53.4 us
    reduce_scatter x1, waiting for transfers between devices, body(): lax.psum_scatter(grad_read_part.astype(jnp.bfloat16), 'head', scatter_dim...  51.8 us
  transfers between devices with their start and end apart: 9, of which 7 were waited for; matrix products, arithmetic and copies ran while one was open for 8% of the time, Pallas kernels for 0%

commit v1 on v0

v1 whole, which is shorter than its diff:
```python
import jax
import jax.numpy as jnp
from jax import lax
from jax.experimental import pallas as pl
from jax.experimental.pallas import tpu as pltpu
from jax.sharding import PartitionSpec as P

BLOCK = 256
F32 = jnp.float32
BF16 = jnp.bfloat16
MESH = pl.DeviceIdType.MESH
HIGH = lax.Precision.HIGHEST
N_TM = 32
N_HEAD = 16
CHIPS = N_TM // 2
NB = 4
NH = 4
CAP = 32


def mm(a, b):
    return lax.dot_general(a, b, (((1,), (0,)), ((), ())), preferred_element_type=F32)


def mm_nt(a, b):
    return lax.dot_general(a, b, (((1,), (1,)), ((), ())), preferred_element_type=F32)


def mm_tn(a, b):
    return lax.dot_general(a, b, (((0,), (0,)), ((), ())), preferred_element_type=F32)


def block_rows(b, size=BLOCK):
    return pl.ds(pl.multiple_of(b * size, size), size)


def kernel(
    x_ref, write_ref, read_ref, decay_ref, weight_ref, cap_ref, start_ref, end_ref,
    gi_ref, gw_ref, gr_ref, gow_ref,
    cgat, cols, meta, meta_prev, zown, zprev, zst, mask, hm,
    ld8, rowrun, growx, fadex, totx, xf, gg, gy, sblk, ablk, decay, scores, cross,
    out_acc, in_acc, wr_acc, entry, leave,
    dev, dev_b, pair_s, pair_a, adj, adj_b, lg, lg_pair, lgt, st_t, ad_t, tot_s, tot_a, ent, ext,
    lay, ppart, pprev, plb, rs_r, rs_w, rr, rw,
    c_s, c_r, cols_s, cols_r, one_s, one_r, lg_s, lg_r, t_s, t_r, a_s, a_r, pl_s, pl_r, rr_s, rr_r, rw_s, rw_r,
):
    me = lax.axis_index("tm")
    z = lax.axis_index("head")
    chip = me // 2
    core = me % 2
    pair = me + 1 - 2 * core
    nxt = (me + 1) % N_TM
    prv = (me + N_TM - 1) % N_TM

    def send(src, dst, s, r, **where):
        return pltpu.make_async_remote_copy(
            src_ref=src, dst_ref=dst, send_sem=s, recv_sem=r, device_id=where, device_id_type=MESH
        )

    barrier = pltpu.get_barrier_semaphore()

    def hail_tm(d, carry):
        pl.semaphore_signal(barrier, inc=1, device_id={"tm": (me + d) % N_TM}, device_id_type=MESH)
        return carry

    def hail_head(d, carry):
        pl.semaphore_signal(barrier, inc=1, device_id={"head": (z + d) % N_HEAD}, device_id_type=MESH)
        return carry

    lax.fori_loop(1, N_TM, hail_tm, 0)
    lax.fori_loop(1, N_HEAD, hail_head, 0)

    cgat[z] = cap_ref[...].astype(BF16)
    spread = (
        lax.broadcasted_iota(jnp.int32, (CAP, 128), 1) % CAP
        == lax.broadcasted_iota(jnp.int32, (CAP, 128), 0)
    ).astype(F32)
    start_f = start_ref[...].astype(F32)
    end_f = end_ref[...].astype(F32)
    start_row = jnp.dot(jnp.broadcast_to(start_f, (8, CAP)), spread, precision=HIGH, preferred_element_type=F32)
    end_row = jnp.dot(jnp.broadcast_to(end_f, (8, CAP)), spread, precision=HIGH, preferred_element_type=F32)
    meta[0] = start_row
    meta[1] = end_row
    eye = lax.broadcasted_iota(jnp.int32, (CAP, CAP), 0) == lax.broadcasted_iota(jnp.int32, (CAP, CAP), 1)
    inv_len = jnp.sum(jnp.where(eye, 1.0 / jnp.maximum(end_f - start_f, 1.0), 0.0), axis=1, keepdims=True)

    pl.semaphore_wait(barrier, N_TM - 1 + N_HEAD - 1)

    for d in (8, 7, 9, 6, 10, 5, 11, 4, 12, 3, 13, 2, 14, 1, 15):
        send(cgat.at[z], cgat.at[z], c_s.at[d], c_r.at[z], head=(z + d) % N_HEAD).start()
    meta_copy = send(meta, meta_prev, one_s.at[0], one_r.at[0], tm=nxt)
    meta_copy.start()

    lane_head = lax.broadcasted_iota(jnp.int32, (BLOCK, BLOCK), 1) // 64
    row_id = lax.broadcasted_iota(jnp.int32, (BLOCK, BLOCK), 0)
    col_id = lax.broadcasted_iota(jnp.int32, (BLOCK, BLOCK), 1)
    for h in range(NH):
        hm[h] = (lane_head == h).astype(F32).astype(BF16)
    tri = (row_id <= col_id).astype(F32)
    ld8[...] = jnp.zeros_like(ld8)
    ld8[0:4, :] = decay_ref[...]

    def local_state(b, carry):
        rows = block_rows(b)
        run = jnp.dot(ld8[:, rows], tri, precision=HIGH, preferred_element_type=F32)
        rowrun[b] = run
        col = run.T
        runx = jnp.where(
            lane_head < 2,
            jnp.where(lane_head < 1, col[:, 0:1], col[:, 1:2]),
            jnp.where(lane_head < 3, col[:, 2:3], col[:, 3:4]),
        )
        total = runx[BLOCK - 1 : BLOCK, :]
        growx[b] = jnp.exp(runx)
        fade = jnp.exp(total - runx)
        fadex[b] = fade
        totx[b] = jnp.broadcast_to(total, (8, BLOCK))
        faded = (x_ref[rows, :].astype(F32) * fade).astype(BF16)
        xf[b] = faded
        sblk[b] = mm_tn(write_ref[rows, :], faded)
        return carry

    lax.fori_loop(0, NB, local_state, 0)

    state = sblk[0]
    for b in range(1, NB):
        state = jnp.exp(totx[b, 0:1, :]) * state + sblk[b]
    log_all = totx[0] + totx[1] + totx[2] + totx[3]
    for half in range(2):
        cut = slice(128 * half, 128 * half + 128)
        dev[half] = state[:, cut]
        dev_b[half] = state[:, cut].astype(BF16)
        lg[half] = log_all[:, cut]
    state_copy = send(dev_b, pair_s, one_s.at[1], one_r.at[1], tm=pair)
    state_copy.start()
    lg_copy = send(lg, lg_pair, one_s.at[2], one_r.at[2], tm=pair)
    lg_copy.start()

    def local_scores(b, carry):
        rows = block_rows(b)
        both = mm_nt(read_ref[rows, :], write_ref[rows, :])
        run = rowrun[b]
        col = run.T
        xb = x_ref[rows, :]
        out = jnp.zeros((BLOCK, BLOCK), F32)
        for h in range(NH):
            gap = col[:, h : h + 1] - run[h : h + 1, :]
            dec = jnp.exp(jnp.where(row_id >= col_id, gap, -jnp.inf))
            decay[b * NH + h] = dec
            sc = (both * dec).astype(BF16)
            scores[b * NH + h] = sc
            out += mm(sc, xb * hm[h])
        out_acc[b] = out
        return carry

    lax.fori_loop(0, 2, local_scores, 0)

    state_copy.wait_recv()
    lg_copy.wait_recv()
    first = core == 0
    log0 = [jnp.where(first, lg[h], lg_pair[h])[0:1, :] for h in range(2)]
    log1 = [jnp.where(first, lg_pair[h], lg[h])[0:1, :] for h in range(2)]

    mine = dev[core]
    other = pair_s[core].astype(F32)
    s0 = jnp.where(first, mine, other)
    s1 = jnp.where(first, other, mine)
    l0 = jnp.where(first, log0[0], log0[1])
    l1 = jnp.where(first, log1[0], log1[1])
    tot_s[...] = (s1 + jnp.exp(l1) * s0).astype(BF16)
    lgt[chip] = jnp.broadcast_to(l0 + l1, (8, 128))

    def send_log(d, carry):
        to = (chip + d) % CHIPS
        send(lgt.at[chip], lgt.at[chip], lg_s.at[to], lg_r.at[chip], tm=to * 2 + core).start()
        return carry

    def send_state(to, carry):
        send(tot_s, st_t.at[chip], t_s.at[to], t_r.at[chip], tm=to * 2 + core).start()
        return carry

    lax.fori_loop(1, CHIPS, send_log, 0)
    lax.fori_loop(chip + 1, CHIPS, send_state, 0)
    lax.fori_loop(2, NB, local_scores, 0)

    proj = mm(cgat[z], weight_ref[block_rows(z, 128), :])
    for d in (1, 15, 2, 14, 3, 13, 4, 12, 5, 11, 6, 10, 7, 9, 8):
        frm = (z + d) % N_HEAD
        send(cgat.at[frm], cgat.at[frm], c_s.at[d], c_r.at[frm], head=frm).wait_recv()
        proj += mm(cgat[frm], weight_ref[block_rows(frm, 128), :])
    proj = proj * inv_len
    zown[...] = proj
    z_copy = send(zown, zprev, one_s.at[3], one_r.at[3], tm=nxt)
    z_copy.start()

    cols[me] = cgat[chip]

    def send_cols(d, carry):
        to = (me + d) % N_TM
        send(cgat.at[to // 2], cols.at[me], cols_s.at[to], cols_r.at[me], tm=to).start()
        return carry

    lax.fori_loop(1, N_TM, send_cols, 0)

    meta_copy.wait_recv()
    lane = lax.broadcasted_iota(jnp.int32, (BLOCK, 128), 1)
    frame = lax.broadcasted_iota(jnp.int32, (BLOCK, 128), 0)
    seg_start = jnp.where(lane[0:8] < 64, meta[0], meta_prev[0])[0:1, :]
    seg_end = jnp.where(lane[0:8] < 64, meta[1], meta_prev[1])[0:1, :]

    def cover(b, carry):
        t = (frame + (me * (NB * BLOCK) + b * BLOCK)).astype(F32)
        inside = jnp.where(t >= seg_start, jnp.where(t < seg_end, 1.0, 0.0), 0.0)
        mask[block_rows(b), :] = inside.astype(BF16)
        return carry

    lax.fori_loop(0, NB, cover, 0)

    def await_log(d, carry):
        frm = (chip + d) % CHIPS
        send(lgt.at[frm], lgt.at[frm], lg_s.at[frm], lg_r.at[frm], tm=frm * 2 + core).wait_recv()
        return carry

    lax.fori_loop(1, CHIPS, await_log, 0)

    def take_state(m, acc):
        send(tot_s, st_t.at[m], t_s.at[m], t_r.at[m], tm=m * 2 + core).wait_recv()
        return jnp.exp(lgt[m][0:1, :]) * acc + st_t[m].astype(F32)

    ent[core] = lax.fori_loop(0, chip, take_state, jnp.zeros((128, 128), F32))
    ent_copy = send(ent.at[core], ent.at[core], one_s.at[4], one_r.at[4 + core], tm=pair)
    ent_copy.start()

    hi = proj.astype(BF16)
    zst[0:32, :] = hi
    zst[32:64, :] = (proj - hi.astype(F32)).astype(BF16)
    z_copy.wait_recv()
    before = zprev[...]
    hi = before.astype(BF16)
    zst[64:96, :] = hi
    zst[96:128, :] = (before - hi.astype(F32)).astype(BF16)

    def local_adjoint(b, carry):
        rows = block_rows(b)
        g = mm(mask[rows, :], zst[...]).astype(BF16)
        gy[b] = g
        grown = (g.astype(F32) * growx[b]).astype(BF16)
        gg[b] = grown
        ablk[b] = mm_tn(read_ref[rows, :], grown)
        return carry

    lax.fori_loop(0, NB, local_adjoint, 0)
    back = ablk[NB - 1]
    for b in range(NB - 2, -1, -1):
        back = jnp.exp(totx[b, 0:1, :]) * back + ablk[b]
    for half in range(2):
        cut = slice(128 * half, 128 * half + 128)
        adj[half] = back[:, cut]
        adj_b[half] = back[:, cut].astype(BF16)
    adj_copy = send(adj_b, pair_a, one_s.at[6], one_r.at[6], tm=pair)
    adj_copy.start()

    send(ent.at[core], ent.at[1 - core], one_s.at[4], one_r.at[5 - core], tm=pair).wait_recv()
    halves = []
    for half in range(2):
        came = ent[half]
        halves.append(jnp.where(first, came, jnp.exp(log0[half]) * came + pair_s[half].astype(F32)))
    carry_state = jnp.concatenate(halves, axis=1)
    for b in range(NB):
        entry[b] = carry_state.astype(BF16)
        if b < NB - 1:
            carry_state = jnp.exp(totx[b, 0:1, :]) * carry_state + sblk[b]

    adj_copy.wait_recv()
    mine = adj[core]
    other = pair_a[core].astype(F32)
    a0 = jnp.where(first, mine, other)
    a1 = jnp.where(first, other, mine)
    tot_a[...] = (a0 + jnp.exp(l0) * a1).astype(BF16)

    def send_adjoint(to, carry):
        send(tot_a, ad_t.at[chip], a_s.at[to], a_r.at[chip], tm=to * 2 + core).start()
        return carry

    lax.fori_loop(0, chip, send_adjoint, 0)

    def pooled(b, acc):
        rows = block_rows(b)
        y = (out_acc[b] + growx[b] * mm(read_ref[rows, :], entry[b])).astype(BF16)
        lay[rows, :] = y
        return acc + mm_tn(mask[rows, :], y)

    pool = lax.fori_loop(0, NB, pooled, jnp.zeros((128, BLOCK), F32))
    ppart[...] = pool[64:96, :]
    p_copy = send(ppart, pprev, one_s.at[7], one_r.at[7], tm=prv)
    p_copy.start()

    def send_part(buf, into, s, r, b):
        for k in range(4):
            to = b * 4 + k

            @pl.when(to != z)
            def _():
                send(buf.at[to], into.at[z], s.at[to], r.at[z], head=to).start()

    def local_cross(i, carry):
        b = (i + z // 4 + 2) % NB
        rows = block_rows(b)
        g = gy[b]
        xb = x_ref[rows, :]
        both = jnp.zeros((BLOCK, BLOCK), F32)
        into = jnp.zeros((BLOCK, BLOCK), F32)
        for h in range(NH):
            gh = g * hm[h]
            both += decay[b * NH + h] * mm_nt(gh, xb)
            into += mm_tn(scores[b * NH + h], gh)
        in_acc[b] = into
        both = both.astype(BF16)
        part = mm(both, write_ref[rows, :]) + mm_nt(gg[b], entry[b])
        for k in range(4):
            rs_r[b * 4 + k] = part[64 * k : 64 * k + 64, :].astype(BF16)
        send_part(rs_r, rr, rr_s, rr_r, b)
        wr_acc[b] = mm_tn(both, read_ref[rows, :])
        return carry

    lax.fori_loop(0, NB, local_cross, 0)

    p_copy.wait_recv()
    plb[me] = ((pool[0:32, :] + pprev[...]) * inv_len).astype(BF16)

    def send_pool(d, carry):
        to = (me + d) % N_TM
        send(plb.at[me], plb.at[me], pl_s.at[to], pl_r.at[me], tm=to).start()
        return carry

    def take_adjoint(i, acc):
        m = CHIPS - 1 - i
        send(tot_a, ad_t.at[m], a_s.at[m], a_r.at[m], tm=m * 2 + core).wait_recv()
        return jnp.exp(lgt[m][0:1, :]) * acc + ad_t[m].astype(F32)

    ext[core] = lax.fori_loop(0, CHIPS - 1 - chip, take_adjoint, jnp.zeros((128, 128), F32))
    ext_copy = send(ext.at[core], ext.at[core], one_s.at[8], one_r.at[8 + core], tm=pair)
    ext_copy.start()
    lax.fori_loop(1, N_TM, send_pool, 0)
    send(ext.at[core], ext.at[1 - core], one_s.at[8], one_r.at[9 - core], tm=pair).wait_recv()
    halves = []
    for half in range(2):
        came = ext[half]
        halves.append(jnp.where(first, jnp.exp(log1[half]) * came + pair_a[half].astype(F32), came))
    carry_adj = jnp.concatenate(halves, axis=1)
    for b in range(NB - 1, -1, -1):
        leave[b] = carry_adj.astype(BF16)
        if b > 0:
            carry_adj = jnp.exp(totx[b, 0:1, :]) * carry_adj + ablk[b]

    def late_write(i, carry):
        b = (i + z // 4 + 2) % NB
        part = wr_acc[b] + mm_nt(xf[b], leave[b])
        for k in range(4):
            rs_w[b * 4 + k] = part[64 * k : 64 * k + 64, :].astype(BF16)
        send_part(rs_w, rw, rw_s, rw_r, b)
        return carry

    lax.fori_loop(0, NB, late_write, 0)

    def late_inputs(b, carry):
        rows = block_rows(b)
        gi_ref[rows, :] = (in_acc[b] + fadex[b] * mm(write_ref[rows, :], leave[b])).astype(BF16)
        return carry

    lax.fori_loop(0, NB, late_inputs, 0)

    def await_pool(d, carry):
        frm = (me + d) % N_TM
        send(cgat.at[0], cols.at[frm], cols_s.at[frm], cols_r.at[frm], tm=frm).wait_recv()
        send(plb.at[frm], plb.at[frm], pl_s.at[frm], pl_r.at[frm], tm=frm).wait_recv()
        return carry

    lax.fori_loop(1, N_TM, await_pool, 0)
    weight_grad = mm_tn(cols[...].reshape(N_TM * CAP, 128), plb[...].reshape(N_TM * CAP, BLOCK))
    gow_ref[...] = jnp.where(first, weight_grad[0:64, :], weight_grad[64:128, :])

    def take(buf, into, s, r):
        def step(d, acc):
            frm = (z + d) % N_HEAD
            send(buf.at[frm], into.at[frm], s.at[frm], r.at[frm], head=frm).wait_recv()
            return acc + into[frm].astype(F32)

        return lax.fori_loop(1, N_HEAD, step, buf[z].astype(F32))

    gr_ref[...] = take(rs_r, rr, rr_s, rr_r)
    gw_ref[...] = take(rs_w, rw, rw_s, rw_r)

    for d in range(1, N_HEAD):
        send(cgat.at[z], cgat.at[z], c_s.at[d], c_r.at[z], head=(z + d) % N_HEAD).wait_send()
    for copy in (meta_copy, state_copy, lg_copy, z_copy, ent_copy, adj_copy, p_copy, ext_copy):
        copy.wait_send()

    def sent_tm(d, carry):
        to = (me + d) % N_TM
        send(cgat.at[0], cols.at[me], cols_s.at[to], cols_r.at[me], tm=to).wait_send()
        send(plb.at[me], plb.at[me], pl_s.at[to], pl_r.at[me], tm=to).wait_send()
        return carry

    def sent_log(d, carry):
        to = (chip + d) % CHIPS
        send(lgt.at[chip], lgt.at[chip], lg_s.at[to], lg_r.at[chip], tm=to * 2 + core).wait_send()
        return carry

    def sent_state(to, carry):
        send(tot_s, st_t.at[chip], t_s.at[to], t_r.at[chip], tm=to * 2 + core).wait_send()
        return carry

    def sent_adjoint(to, carry):
        send(tot_a, ad_t.at[chip], a_s.at[to], a_r.at[chip], tm=to * 2 + core).wait_send()
        return carry

    def sent_head(d, carry):
        to = (z + d) % N_HEAD
        send(rs_r.at[to], rr.at[z], rr_s.at[to], rr_r.at[z], head=to).wait_send()
        send(rs_w.at[to], rw.at[z], rw_s.at[to], rw_r.at[z], head=to).wait_send()
        return carry

    lax.fori_loop(1, N_TM, sent_tm, 0)
    lax.fori_loop(1, CHIPS, sent_log, 0)
    lax.fori_loop(chip + 1, CHIPS, sent_state, 0)
    lax.fori_loop(0, chip, sent_adjoint, 0)
    lax.fori_loop(1, N_HEAD, sent_head, 0)


def body(frame_inputs, write_map, read_map, log_decay, out_weight, caption_grad, caption_start, caption_end):
    frames, width = frame_inputs.shape
    V = pltpu.VMEM
    DMA = pltpu.SemaphoreType.DMA
    state = (2, 128, 128)
    tile = (BLOCK, BLOCK)
    scratch = [
        V((N_HEAD, CAP, 128), BF16),
        V((N_TM, CAP, 128), BF16),
        V((2, 8, 128), F32),
        V((2, 8, 128), F32),
        V((CAP, BLOCK), F32),
        V((CAP, BLOCK), F32),
        V((128, BLOCK), BF16),
        V((frames, 128), BF16),
        V((NH, *tile), BF16),
        V((8, frames), F32),
        V((NB, 8, BLOCK), F32),
        V((NB, *tile), F32),
        V((NB, *tile), F32),
        V((NB, 8, BLOCK), F32),
        V((NB, *tile), BF16),
        V((NB, *tile), BF16),
        V((NB, *tile), BF16),
        V((NB, 128, BLOCK), F32),
        V((NB, 128, BLOCK), F32),
        V((NB * NH, *tile), F32),
        V((NB * NH, *tile), BF16),
        V((8, 128), BF16),
        V((NB, *tile), F32),
        V((NB, *tile), F32),
        V((NB, BLOCK, 128), F32),
        V((NB, 128, BLOCK), BF16),
        V((NB, 128, BLOCK), BF16),
        V(state, F32),
        V(state, BF16),
        V(state, BF16),
        V(state, BF16),
        V(state, F32),
        V(state, BF16),
        V((2, 8, 128), F32),
        V((2, 8, 128), F32),
        V((CHIPS, 8, 128), F32),
        V((CHIPS, 128, 128), BF16),
        V((CHIPS, 128, 128), BF16),
        V((128, 128), BF16),
        V((128, 128), BF16),
        V(state, F32),
        V(state, F32),
        V((frames, BLOCK), BF16),
        V((CAP, BLOCK), F32),
        V((CAP, BLOCK), F32),
        V((N_TM, CAP, BLOCK), BF16),
        V((N_HEAD, 64, 128), BF16),
        V((N_HEAD, 64, 128), BF16),
        V((N_HEAD, 64, 128), BF16),
        V((N_HEAD, 64, 128), BF16),
        DMA((N_HEAD,)),
        DMA((N_HEAD,)),
        DMA((N_TM,)),
        DMA((N_TM,)),
        DMA((10,)),
        DMA((10,)),
        DMA((CHIPS,)),
        DMA((CHIPS,)),
        DMA((CHIPS,)),
        DMA((CHIPS,)),
        DMA((CHIPS,)),
        DMA((CHIPS,)),
        DMA((N_TM,)),
        DMA((N_TM,)),
        DMA((N_HEAD,)),
        DMA((N_HEAD,)),
        DMA((N_HEAD,)),
        DMA((N_HEAD,)),
    ]
    vmem = pl.BlockSpec(memory_space=pltpu.VMEM)
    return pl.pallas_call(
        kernel,
        out_shape=(
            jax.ShapeDtypeStruct((frames, width), BF16),
            jax.ShapeDtypeStruct((64, 128), F32),
            jax.ShapeDtypeStruct((64, 128), F32),
            jax.ShapeDtypeStruct((64, BLOCK), F32),
        ),
        in_specs=[vmem] * 8,
        out_specs=(vmem,) * 4,
        scratch_shapes=scratch,
        compiler_params=pltpu.CompilerParams(
            collective_id=0, has_side_effects=True, vmem_limit_bytes=48 * 1024 * 1024
        ),
    )(
        frame_inputs, write_map, read_map, log_decay, out_weight, caption_grad,
        caption_start.reshape(1, CAP), caption_end.reshape(1, CAP),
    )


def solution(mesh):
    in_specs = (
        P("tm", "head"),
        P("tm", None),
        P("tm", None),
        P("head", "tm"),
        P(None, "head"),
        P("tm", "head"),
        P("tm"),
        P("tm"),
    )
    out_specs = (P("tm", "head"), P(("tm", "head"), None), P(("tm", "head"), None), P("tm", "head"))
    return jax.shard_map(body, mesh=mesh, in_specs=in_specs, out_specs=out_specs, check_vma=False)
```

time: 509 us -> 73.9 us (0.15)
  waiting for transfers between devices: 366 us -> 0 us
  Pallas kernels: 0 us -> 63.3 us
  blocking collectives: 53.4 us -> 0 us
  matrix products: 29.5 us -> 0 us
  other arithmetic: 21.7 us -> 0 us
  between operations: 15.3 us -> 0.67 us
  starting transfers between devices: 7.75 us -> 0 us
  local copies, waits for them, and re-layouts: 14.1 us -> 8.91 us
    reduce_scatter x3 -> x0, waiting for transfers between devices: 221 us -> none  [the longest x1 101 us: body(): lax.psum_scatter(lax.dot_general(frame_grad, layer_out, (((0,), (0,)), ((...]
    all_gather x3 -> x0, waiting for transfers between devices: 139 us -> none  [the longest x1 85.6 us: body(): frame_grad = lax.all_gather(local_grad, 'head', axis=1, tiled=True)]
    pallas_call x0 -> x1, Pallas kernels: none -> 63.3 us  [body(): pl.pallas_call(kernel, out_shape=(jax.ShapeDtypeStruct((frames, width), B...]
    unnamed x1 -> x0, blocking collectives: 53.4 us -> none
    dot_general x15 -> x0, matrix products: 29.5 us -> none  [the longest x1 4.23 us: body(): jnp.dot(frame_grad, out_weight, preferred_element_type=jnp.float32)]
    convert_element_type x8 -> x0, other arithmetic: 7.32 us -> none  [the longest x2 2.67 us: body(): grad_write, grad_read = (lax.psum_scatter(grad_write_part.astype(jnp.bflo...]
    ppermute x3 -> x0, starting transfers between devices: 7.32 us -> none  [from_behind(): return lax.ppermute(shard, axis, pairs)]
    reshape x5 -> x0, local copies, waits for them, and re-layouts: 6.61 us -> none  [the longest x2 3.3 us: body(): grads = grad_y.reshape(block_count, BLOCK, head_count, head_size)]
  transfers between devices with their start and end apart: 9 -> 0, of which waited for: 7 -> 0; matrix products, arithmetic and copies ran while one was open for 8% -> 0% of each run, Pallas kernels for 0% -> 0%
where the time goes in v1:
time: 73.9 us; the launch traced here: 72.9 us
  Pallas kernels  63.3 us (86%)
  local copies, waits for them, and re-layouts  8.91 us (12%)
    pallas_call x1, Pallas kernels, body(): pl.pallas_call(kernel, out_shape=(jax.ShapeDtypeStruct((frames, width), B...  63.3 us
    unnamed x20, local copies, waits for them, and re-layouts  8.91 us

profile of v1, /device:TPU:24, one launch (start us, length us, event | category | flops | bytes accessed | tf_op | source)
XLA Modules:
  0.0 72.9 jit_solution(490497893173548746)
XLA Ops:
  0.6 0.0 copy-start.6
  0.6 0.0 copy-start.7
  0.7 0.6 copy-done.6
  1.3 0.0 copy-done.7
  1.3 0.0 copy-start
  1.3 1.2 %copy-done = bf16[2048,256]{1,0:T(8,128)(2,1)S(1)} copy-done((bf16[2048,256]{1,0:T(8,128)(2,1)S(1)}, bf16[2048,256]{1,0:T(8,128)(2,1)}, u32[]{:S(2)}) %copy-start) | copy-done | bytes 1048600
  2.5 0.0 copy-start.1
  2.5 1.0 %copy-done.1 = bf16[1024,256]{1,0:T(8,128)(2,1)S(1)} copy-done((bf16[1024,256]{1,0:T(8,128)(2,1)S(1)}, bf16[1024,256]{1,0:T(8,128)(2,1)}, u32[]{:S(2)}) %copy-start.1) | copy-done | bytes 524312
  3.6 0.0 copy-start.2
  3.6 0.9 %copy-done.2 = bf16[1024,128]{1,0:T(8,128)(2,1)S(1)} copy-done((bf16[1024,128]{1,0:T(8,128)(2,1)S(1)}, bf16[1024,128]{1,0:T(8,128)(2,1)}, u32[]{:S(2)}) %copy-start.2) | copy-done | bytes 262168
  4.5 0.0 copy-start.3
  4.5 0.9 %copy-done.3 = bf16[1024,128]{1,0:T(8,128)(2,1)S(1)} copy-done((bf16[1024,128]{1,0:T(8,128)(2,1)S(1)}, bf16[1024,128]{1,0:T(8,128)(2,1)}, u32[]{:S(2)}) %copy-start.3) | copy-done | bytes 262168
  5.5 0.0 copy-start.4
  5.5 0.7 copy-done.4
  6.2 0.0 copy-start.5
  6.2 0.7 copy-done.5
  6.9 63.3 %shard_map.111 = (bf16[1024,256]{1,0:T(8,128)(2,1)S(1)}, f32[64,128]{1,0:T(8,128)S(1)}, f32[64,128]{1,0:T(8,128)S(1)}, f32[64,256]{1,0:T(8,128)S(1)}) custom-call(bf16[1024,256]{1,0:T(8,128)(2,1)S(1)} %copy-done.1, bf16[1024,128]{1,0:T(8,128)(2,1)S(1)} %copy-done.2, bf16[1024,128]{1,0:T(8,128)(2,1)S(1)} %copy-done.3, f32[4,1024]{1,0:T(4,128)S(1)} %copy-done.4, ...), custom_call_target="tpu_custom_call" | custom-call | tf_op jit(solution)/shard_map/pallas_call | solution.py:508
  70.2 0.8 %copy.16 = bf16[1024,256]{1,0:T(8,128)(2,1)} copy(bf16[1024,256]{1,0:T(8,128)(2,1)S(1)} %get-tuple-element.8) | data formatting | bytes 1048576
  71.0 0.6 copy.17
  71.6 0.6 copy.18
  72.2 0.6 copy.19
Async XLA Ops:
  0.6 0.7 copy-start.6
  0.6 0.7 copy-start.7
  1.3 1.2 %copy-start = (bf16[2048,256]{1,0:T(8,128)(2,1)S(1)}, bf16[2048,256]{1,0:T(8,128)(2,1)}, u32[]{:S(2)}) copy-start(bf16[2048,256]{1,0:T(8,128)(2,1)} %weight_ref.1) | copy-start | bytes 3145732
  2.5 1.0 %copy-start.1 = (bf16[1024,256]{1,0:T(8,128)(2,1)S(1)}, bf16[1024,256]{1,0:T(8,128)(2,1)}, u32[]{:S(2)}) copy-start(bf16[1024,256]{1,0:T(8,128)(2,1)} %x_ref.1) | copy-start | bytes 1572868
  3.6 0.9 %copy-start.2 = (bf16[1024,128]{1,0:T(8,128)(2,1)S(1)}, bf16[1024,128]{1,0:T(8,128)(2,1)}, u32[]{:S(2)}) copy-start(bf16[1024,128]{1,0:T(8,128)(2,1)} %write_ref.1) | copy-start | bytes 786436
  4.5 0.9 %copy-start.3 = (bf16[1024,128]{1,0:T(8,128)(2,1)S(1)}, bf16[1024,128]{1,0:T(8,128)(2,1)}, u32[]{:S(2)}) copy-start(bf16[1024,128]{1,0:T(8,128)(2,1)} %read_ref.1) | copy-start | bytes 786436
  5.5 0.7 copy-start.4
  6.2 0.7 copy-start.5

commit v2 on v1

--- a/solution.py
+++ b/solution.py
@@ -35,14 +35,15 @@
 
 
 def kernel(
-    x_ref, write_ref, read_ref, decay_ref, weight_ref, cap_ref, start_ref, end_ref,
+    x_hbm, write_hbm, read_hbm, decay_hbm, weight_hbm, cap_hbm, start_hbm, end_hbm,
     gi_ref, gw_ref, gr_ref, gow_ref,
+    x_ref, write_ref, read_ref, decay_ref, weight_ref, cap_ref, start_ref, end_ref, in_s,
     cgat, cols, meta, meta_prev, zown, zprev, zst, mask, hm,
-    ld8, rowrun, growx, fadex, totx, xf, gg, gy, sblk, ablk, decay, scores, cross,
+    ld8, rowrun, growx, fadex, totx, xf, gg, gy, sblk, ablk, decay, scores,
     out_acc, in_acc, wr_acc, entry, leave,
     dev, dev_b, pair_s, pair_a, adj, adj_b, lg, lg_pair, lgt, st_t, ad_t, tot_s, tot_a, ent, ext,
-    lay, ppart, pprev, plb, rs_r, rs_w, rr, rw,
-    c_s, c_r, cols_s, cols_r, one_s, one_r, lg_s, lg_r, t_s, t_r, a_s, a_r, pl_s, pl_r, rr_s, rr_r, rw_s, rw_r,
+    ppart, pprev, plb, rs_r, rs_w, mid_r, mid_w, rr, rw, gi_vm,
+    c_s, c_r, cols_s, cols_r, one_s, one_r, lg_s, lg_r, t_s, t_r, a_s, a_r, pl_s, pl_r, rr_s, rr_r, rw_s, rw_r, mid_r_s, mid_w_s,
 ):
     me = lax.axis_index("tm")
     z = lax.axis_index("head")
@@ -57,6 +58,23 @@
             src_ref=src, dst_ref=dst, send_sem=s, recv_sem=r, device_id=where, device_id_type=MESH
         )
 
+    fetch = [
+        pltpu.make_async_copy(src, dst, in_s.at[i])
+        for i, (src, dst) in enumerate(
+            (
+                (cap_hbm, cap_ref),
+                (start_hbm, start_ref),
+                (end_hbm, end_ref),
+                (decay_hbm, decay_ref),
+                (x_hbm, x_ref),
+                (write_hbm, write_ref),
+                (read_hbm, read_ref),
+                (weight_hbm, weight_ref),
+            )
+        )
+    ]
+    for copy in fetch:
+        copy.start()
     barrier = pltpu.get_barrier_semaphore()
 
     def hail_tm(d, carry):
@@ -70,6 +88,8 @@
     lax.fori_loop(1, N_TM, hail_tm, 0)
     lax.fori_loop(1, N_HEAD, hail_head, 0)
 
+    for copy in fetch[:3]:
+        copy.wait()
     cgat[z] = cap_ref[...].astype(BF16)
     spread = (
         lax.broadcasted_iota(jnp.int32, (CAP, 128), 1) % CAP
@@ -98,7 +118,10 @@
         hm[h] = (lane_head == h).astype(F32).astype(BF16)
     tri = (row_id <= col_id).astype(F32)
     ld8[...] = jnp.zeros_like(ld8)
+    fetch[3].wait()
     ld8[0:4, :] = decay_ref[...]
+    fetch[4].wait()
+    fetch[5].wait()
 
     def local_state(b, carry):
         rows = block_rows(b)
@@ -136,6 +159,8 @@
     lg_copy = send(lg, lg_pair, one_s.at[2], one_r.at[2], tm=pair)
     lg_copy.start()
 
+    fetch[6].wait()
+
     def local_scores(b, carry):
         rows = block_rows(b)
         both = mm_nt(read_ref[rows, :], write_ref[rows, :])
@@ -183,6 +208,7 @@
     lax.fori_loop(chip + 1, CHIPS, send_state, 0)
     lax.fori_loop(2, NB, local_scores, 0)
 
+    fetch[7].wait()
     proj = mm(cgat[z], weight_ref[block_rows(z, 128), :])
     for d in (1, 15, 2, 14, 3, 13, 4, 12, 5, 11, 6, 10, 7, 9, 8):
         frm = (z + d) % N_HEAD
@@ -234,13 +260,10 @@
     hi = proj.astype(BF16)
     zst[0:32, :] = hi
     zst[32:64, :] = (proj - hi.astype(F32)).astype(BF16)
-    z_copy.wait_recv()
-    before = zprev[...]
-    hi = before.astype(BF16)
-    zst[64:96, :] = hi
-    zst[96:128, :] = (before - hi.astype(F32)).astype(BF16)
-
-    def local_adjoint(b, carry):
+    zst[64:128, :] = jnp.zeros((64, BLOCK), BF16)
+
+    def local_adjoint(i, carry):
+        b = NB - 1 - i
         rows = block_rows(b)
         g = mm(mask[rows, :], zst[...]).astype(BF16)
         gy[b] = g
@@ -249,7 +272,13 @@
         ablk[b] = mm_tn(read_ref[rows, :], grown)
         return carry
 
-    lax.fori_loop(0, NB, local_adjoint, 0)
+    lax.fori_loop(0, NB - 1, local_adjoint, 0)
+    z_copy.wait_recv()
+    before = zprev[...]
+    hi = before.astype(BF16)
+    zst[64:96, :] = hi
+    zst[96:128, :] = (before - hi.astype(F32)).astype(BF16)
+    lax.fori_loop(NB - 1, NB, local_adjoint, 0)
     back = ablk[NB - 1]
     for b in range(NB - 2, -1, -1):
         back = jnp.exp(totx[b, 0:1, :]) * back + ablk[b]
@@ -284,27 +313,26 @@
 
     lax.fori_loop(0, chip, send_adjoint, 0)
 
-    def pooled(b, acc):
-        rows = block_rows(b)
-        y = (out_acc[b] + growx[b] * mm(read_ref[rows, :], entry[b])).astype(BF16)
-        lay[rows, :] = y
-        return acc + mm_tn(mask[rows, :], y)
-
-    pool = lax.fori_loop(0, NB, pooled, jnp.zeros((128, BLOCK), F32))
-    ppart[...] = pool[64:96, :]
-    p_copy = send(ppart, pprev, one_s.at[7], one_r.at[7], tm=prv)
-    p_copy.start()
-
-    def send_part(buf, into, s, r, b):
+    def hand_on(buf, mid, s, r, b):
         for k in range(4):
             to = b * 4 + k
-
-            @pl.when(to != z)
+            off = (to - z + N_HEAD) % N_HEAD
+
+            @pl.when((off % 2 == 0) & (off > 0))
             def _():
-                send(buf.at[to], into.at[z], s.at[to], r.at[z], head=to).start()
+                near = (z + 1 - 2 * (off // 9) + N_HEAD) % N_HEAD
+                send(buf.at[to], mid.at[to], s.at[to], r.at[to], head=near).start()
+
+    def send_sums(buf, mid, into, s, m, r):
+        for off in (7, 9, 5, 11, 3, 13, 1, 15):
+            to = (z + off) % N_HEAD
+            if off != 9:
+                send(buf.at[to], mid.at[to], s.at[to], m.at[to], head=to).wait_recv()
+                buf[to] = (buf[to].astype(F32) + mid[to].astype(F32)).astype(BF16)
+            send(buf.at[to], into.at[z], s.at[to], r.at[z], head=to).start()
 
     def local_cross(i, carry):
-        b = (i + z // 4 + 2) % NB
+        b = i
         rows = block_rows(b)
         g = gy[b]
         xb = x_ref[rows, :]
@@ -319,11 +347,24 @@
         part = mm(both, write_ref[rows, :]) + mm_nt(gg[b], entry[b])
         for k in range(4):
             rs_r[b * 4 + k] = part[64 * k : 64 * k + 64, :].astype(BF16)
-        send_part(rs_r, rr, rr_s, rr_r, b)
+        hand_on(rs_r, mid_r, rr_s, mid_r_s, b)
         wr_acc[b] = mm_tn(both, read_ref[rows, :])
         return carry
 
     lax.fori_loop(0, NB, local_cross, 0)
+
+    def pooled(b, acc):
+        rows = block_rows(b)
+        y = (out_acc[b] + growx[b] * mm(read_ref[rows, :], entry[b])).astype(BF16)
+        return acc + mm_tn(mask[rows, :], y)
+
+    pool = pooled(0, jnp.zeros((128, BLOCK), F32))
+    ppart[...] = pool[64:96, :]
+    p_copy = send(ppart, pprev, one_s.at[7], one_r.at[7], tm=prv)
+    p_copy.start()
+    pool = lax.fori_loop(1, NB, pooled, pool)
+
+    send_sums(rs_r, mid_r, rr, rr_s, mid_r_s, rr_r)
 
     p_copy.wait_recv()
     plb[me] = ((pool[0:32, :] + pprev[...]) * inv_len).astype(BF16)
@@ -354,21 +395,24 @@
             carry_adj = jnp.exp(totx[b, 0:1, :]) * carry_adj + ablk[b]
 
     def late_write(i, carry):
-        b = (i + z // 4 + 2) % NB
+        b = i
         part = wr_acc[b] + mm_nt(xf[b], leave[b])
         for k in range(4):
             rs_w[b * 4 + k] = part[64 * k : 64 * k + 64, :].astype(BF16)
-        send_part(rs_w, rw, rw_s, rw_r, b)
+        hand_on(rs_w, mid_w, rw_s, mid_w_s, b)
         return carry
 
     lax.fori_loop(0, NB, late_write, 0)
 
     def late_inputs(b, carry):
         rows = block_rows(b)
-        gi_ref[rows, :] = (in_acc[b] + fadex[b] * mm(write_ref[rows, :], leave[b])).astype(BF16)
+        gi_vm[rows, :] = (in_acc[b] + fadex[b] * mm(write_ref[rows, :], leave[b])).astype(BF16)
         return carry
 
     lax.fori_loop(0, NB, late_inputs, 0)
+    gi_copy = pltpu.make_async_copy(gi_vm, gi_ref, in_s.at[8])
+    gi_copy.start()
+    send_sums(rs_w, mid_w, rw, rw_s, mid_w_s, rw_r)
 
     def await_pool(d, carry):
         frm = (me + d) % N_TM
@@ -381,15 +425,16 @@
     gow_ref[...] = jnp.where(first, weight_grad[0:64, :], weight_grad[64:128, :])
 
     def take(buf, into, s, r):
-        def step(d, acc):
-            frm = (z + d) % N_HEAD
+        def step(i, acc):
+            frm = (z + 2 * i + 1) % N_HEAD
             send(buf.at[frm], into.at[frm], s.at[frm], r.at[frm], head=frm).wait_recv()
             return acc + into[frm].astype(F32)
 
-        return lax.fori_loop(1, N_HEAD, step, buf[z].astype(F32))
+        return lax.fori_loop(0, N_HEAD // 2, step, buf[z].astype(F32))
 
     gr_ref[...] = take(rs_r, rr, rr_s, rr_r)
     gw_ref[...] = take(rs_w, rw, rw_s, rw_r)
+    gi_copy.wait()
 
     for d in range(1, N_HEAD):
         send(cgat.at[z], cgat.at[z], c_s.at[d], c_r.at[z], head=(z + d) % N_HEAD).wait_send()
@@ -426,6 +471,14 @@
     lax.fori_loop(chip + 1, CHIPS, sent_state, 0)
     lax.fori_loop(0, chip, sent_adjoint, 0)
     lax.fori_loop(1, N_HEAD, sent_head, 0)
+
+
+def write_out(*refs):
+    copies = [pltpu.make_async_copy(refs[i], refs[4 + i], refs[8].at[i]) for i in range(4)]
+    for copy in copies:
+        copy.start()
+    for copy in copies:
+        copy.wait()
 
 
 def body(frame_inputs, write_map, read_map, log_decay, out_weight, caption_grad, caption_start, caption_end):
@@ -435,6 +488,15 @@
     state = (2, 128, 128)
     tile = (BLOCK, BLOCK)
     scratch = [
+        V(frame_inputs.shape, BF16),
+        V(write_map.shape, BF16),
+        V(read_map.shape, BF16),
+        V(log_decay.shape, F32),
+        V(out_weight.shape, BF16),
+        V(caption_grad.shape, F32),
+        V((1, CAP), jnp.int32),
+        V((1, CAP), jnp.int32),
+        DMA((9,)),
         V((N_HEAD, CAP, 128), BF16),
         V((N_TM, CAP, 128), BF16),
         V((2, 8, 128), F32),
@@ -456,7 +518,6 @@
         V((NB, 128, BLOCK), F32),
         V((NB * NH, *tile), F32),
         V((NB * NH, *tile), BF16),
-        V((8, 128), BF16),
         V((NB, *tile), F32),
         V((NB, *tile), F32),
         V((NB, BLOCK, 128), F32),
@@ -477,7 +538,6 @@
         V((128, 128), BF16),
         V(state, F32),
         V(state, F32),
-        V((frames, BLOCK), BF16),
         V((CAP, BLOCK), F32),
         V((CAP, BLOCK), F32),
         V((N_TM, CAP, BLOCK), BF16),
@@ -485,6 +545,9 @@
         V((N_HEAD, 64, 128), BF16),
         V((N_HEAD, 64, 128), BF16),
         V((N_HEAD, 64, 128), BF16),
+        V((N_HEAD, 64, 128), BF16),
+        V((N_HEAD, 64, 128), BF16),
+        V(frame_inputs.shape, BF16),
         DMA((N_HEAD,)),
         DMA((N_HEAD,)),
         DMA((N_TM,)),
@@ -503,9 +566,11 @@
         DMA((N_HEAD,)),
         DMA((N_HEAD,)),
         DMA((N_HEAD,)),
+        DMA((N_HEAD,)),
+        DMA((N_HEAD,)),
     ]
     vmem = pl.BlockSpec(memory_space=pltpu.VMEM)
-    return pl.pallas_call(
+    results = pl.pallas_call(
         kernel,
         out_shape=(
             jax.ShapeDtypeStruct((frames, width), BF16),
@@ -513,16 +578,24 @@
             jax.ShapeDtypeStruct((64, 128), F32),
             jax.ShapeDtypeStruct((64, BLOCK), F32),
         ),
-        in_specs=[vmem] * 8,
-        out_specs=(vmem,) * 4,
+        in_specs=[pl.BlockSpec(memory_space=pltpu.HBM)] * 8,
+        out_specs=(pl.BlockSpec(memory_space=pltpu.HBM), vmem, vmem, vmem),
         scratch_shapes=scratch,
         compiler_params=pltpu.CompilerParams(
-            collective_id=0, has_side_effects=True, vmem_limit_bytes=48 * 1024 * 1024
+            collective_id=0, has_side_effects=True, vmem_limit_bytes=63 * 1024 * 1024
         ),
     )(
         frame_inputs, write_map, read_map, log_decay, out_weight, caption_grad,
         caption_start.reshape(1, CAP), caption_end.reshape(1, CAP),
     )
+    return pl.pallas_call(
+        write_out,
+        out_shape=tuple(jax.ShapeDtypeStruct(r.shape, r.dtype) for r in results),
+        in_specs=[vmem] * 4,
+        out_specs=(pl.BlockSpec(memory_space=pl.ANY),) * 4,
+        scratch_shapes=[DMA((4,))],
+        compiler_params=pltpu.CompilerParams(vmem_limit_bytes=62 * 1024 * 1024),
+    )(*results)
 
 
 def solution(mesh):

time: 73.9 us -> 63.7 us (0.86); the launches traced: 72.9 us -> 63.6 us
  local copies, waits for them, and re-layouts: 8.91 us -> 0 us
    unnamed x20 -> x0, local copies, waits for them, and re-layouts: 8.91 us -> none
    pallas_call x1, Pallas kernels: 63.3 us -> 61 us  [body(): pl.pallas_call(kernel, out_shape=(jax.ShapeDtypeStruct((frames, width), B...]
    pallas_call x0 -> x1, Pallas kernels: none -> 1.93 us  [body(): pl.pallas_call(write_out, out_shape=tuple((jax.ShapeDtypeStruct(r.shape,...]
where the time goes in v2:
time: 63.7 us; the launch traced here: 63.6 us
  Pallas kernels  62.9 us (99%)
  between operations  0.64 us (1%)
    pallas_call x1, Pallas kernels, body(): pl.pallas_call(kernel, out_shape=(jax.ShapeDtypeStruct((frames, width), B...  61 us
    pallas_call x1, Pallas kernels, body(): pl.pallas_call(write_out, out_shape=tuple((jax.ShapeDtypeStruct(r.shape,...  1.93 us

profile of v2, /device:TPU:24, one launch (start us, length us, event | category | flops | bytes accessed | tf_op | source)
XLA Modules:
  0.0 63.6 jit_solution(3482335298687763670)
XLA Ops:
  0.6 61.0 %shard_map.111 = (bf16[1024,256]{1,0:T(8,128)(2,1)}, f32[64,128]{1,0:T(8,128)}, f32[64,128]{1,0:T(8,128)}, f32[64,256]{1,0:T(8,128)}) custom-call(bf16[1024,256]{1,0:T(8,128)(2,1)} %x_hbm.1, bf16[1024,128]{1,0:T(8,128)(2,1)} %write_hbm.1, bf16[1024,128]{1,0:T(8,128)(2,1)} %read_hbm.1, f32[4,1024]{1,0:T(4,128)} %decay_hbm.1, bf16[2048,256]{1,0:T(8,128)(2,1)} %weight_hbm.1, ...), custom_call_target="tpu_custom_call" | custom-call | tf_op jit(solution)/shard_map/pallas_call | solution.py:573
  61.7 1.9 %shard_map.112 = (bf16[1024,256]{1,0:T(8,128)(2,1)}, f32[64,128]{1,0:T(8,128)}, f32[64,128]{1,0:T(8,128)}, f32[64,256]{1,0:T(8,128)}) custom-call(bf16[1024,256]{1,0:T(8,128)(2,1)} %get-tuple-element.8.refs_0_, f32[64,128]{1,0:T(8,128)} %get-tuple-element.9.refs_1_, f32[64,128]{1,0:T(8,128)} %get-tuple-element.10.refs_2_, f32[64,256]{1,0:T(8,128)} %get-tuple-element.11.refs_3_), custom_call_target="tpu_custom_call" | custom-call | tf_op jit(solution)/shard_map/pallas_call | solution.py:591

commit v3 on v2

--- a/solution.py
+++ b/solution.py
@@ -16,6 +16,7 @@
 NB = 4
 NH = 4
 CAP = 32
+FAR_FIRST = (8, 7, 9, 6, 10, 5, 11, 4, 12, 3, 13, 2, 14, 1, 15)
 
 
 def mm(a, b):
@@ -40,9 +41,10 @@
     x_ref, write_ref, read_ref, decay_ref, weight_ref, cap_ref, start_ref, end_ref, in_s,
     cgat, cols, meta, meta_prev, zown, zprev, zst, mask, hm,
     ld8, rowrun, growx, fadex, totx, xf, gg, gy, sblk, ablk, decay, scores,
-    out_acc, in_acc, wr_acc, entry, leave,
+    out_acc, wr_acc, entry, leave,
     dev, dev_b, pair_s, pair_a, adj, adj_b, lg, lg_pair, lgt, st_t, ad_t, tot_s, tot_a, ent, ext,
-    ppart, pprev, plb, rs_r, rs_w, mid_r, mid_w, rr, rw, gi_vm,
+    next_read, next_run, grow_next, spill, spill_adj,
+    ppart, pprev, plb, rs_r, rs_w, mid_r, mid_w, rr, rw, gi_vm, gw_vm, gr_vm, gow_vm,
     c_s, c_r, cols_s, cols_r, one_s, one_r, lg_s, lg_r, t_s, t_r, a_s, a_r, pl_s, pl_r, rr_s, rr_r, rw_s, rw_r, mid_r_s, mid_w_s,
 ):
     me = lax.axis_index("tm")
@@ -73,7 +75,7 @@
             )
         )
     ]
-    for copy in fetch:
+    for copy in fetch[:7]:
         copy.start()
     barrier = pltpu.get_barrier_semaphore()
 
@@ -85,38 +87,16 @@
         pl.semaphore_signal(barrier, inc=1, device_id={"head": (z + d) % N_HEAD}, device_id_type=MESH)
         return carry
 
+    for d in FAR_FIRST:
+        hail_head(d, 0)
     lax.fori_loop(1, N_TM, hail_tm, 0)
-    lax.fori_loop(1, N_HEAD, hail_head, 0)
-
-    for copy in fetch[:3]:
-        copy.wait()
-    cgat[z] = cap_ref[...].astype(BF16)
-    spread = (
-        lax.broadcasted_iota(jnp.int32, (CAP, 128), 1) % CAP
-        == lax.broadcasted_iota(jnp.int32, (CAP, 128), 0)
-    ).astype(F32)
-    start_f = start_ref[...].astype(F32)
-    end_f = end_ref[...].astype(F32)
-    start_row = jnp.dot(jnp.broadcast_to(start_f, (8, CAP)), spread, precision=HIGH, preferred_element_type=F32)
-    end_row = jnp.dot(jnp.broadcast_to(end_f, (8, CAP)), spread, precision=HIGH, preferred_element_type=F32)
-    meta[0] = start_row
-    meta[1] = end_row
-    eye = lax.broadcasted_iota(jnp.int32, (CAP, CAP), 0) == lax.broadcasted_iota(jnp.int32, (CAP, CAP), 1)
-    inv_len = jnp.sum(jnp.where(eye, 1.0 / jnp.maximum(end_f - start_f, 1.0), 0.0), axis=1, keepdims=True)
-
-    pl.semaphore_wait(barrier, N_TM - 1 + N_HEAD - 1)
-
-    for d in (8, 7, 9, 6, 10, 5, 11, 4, 12, 3, 13, 2, 14, 1, 15):
-        send(cgat.at[z], cgat.at[z], c_s.at[d], c_r.at[z], head=(z + d) % N_HEAD).start()
-    meta_copy = send(meta, meta_prev, one_s.at[0], one_r.at[0], tm=nxt)
-    meta_copy.start()
 
     lane_head = lax.broadcasted_iota(jnp.int32, (BLOCK, BLOCK), 1) // 64
     row_id = lax.broadcasted_iota(jnp.int32, (BLOCK, BLOCK), 0)
     col_id = lax.broadcasted_iota(jnp.int32, (BLOCK, BLOCK), 1)
     for h in range(NH):
         hm[h] = (lane_head == h).astype(F32).astype(BF16)
-    tri = (row_id <= col_id).astype(F32)
+    tri = (row_id <= col_id).astype(F32).astype(BF16)
     ld8[...] = jnp.zeros_like(ld8)
     fetch[3].wait()
     ld8[0:4, :] = decay_ref[...]
@@ -125,7 +105,12 @@
 
     def local_state(b, carry):
         rows = block_rows(b)
-        run = jnp.dot(ld8[:, rows], tri, precision=HIGH, preferred_element_type=F32)
+        left = ld8[:, rows]
+        run = jnp.zeros((8, BLOCK), F32)
+        for _ in range(3):
+            part = left.astype(BF16)
+            run += mm(part, tri)
+            left = left - part.astype(F32)
         rowrun[b] = run
         col = run.T
         runx = jnp.where(
@@ -154,12 +139,41 @@
         dev[half] = state[:, cut]
         dev_b[half] = state[:, cut].astype(BF16)
         lg[half] = log_all[:, cut]
+
+    fetch[0].wait()
+    cgat[z] = cap_ref[...].astype(BF16)
+
+    pl.semaphore_wait(barrier, N_TM - 1 + N_HEAD - 1)
+    for d in FAR_FIRST:
+        send(cgat.at[z], cgat.at[z], c_s.at[d], c_r.at[z], head=(z + d) % N_HEAD).start()
     state_copy = send(dev_b, pair_s, one_s.at[1], one_r.at[1], tm=pair)
     state_copy.start()
     lg_copy = send(lg, lg_pair, one_s.at[2], one_r.at[2], tm=pair)
     lg_copy.start()
-
+    fetch[7].start()
     fetch[6].wait()
+    rows_copy = send(read_ref.at[pl.ds(0, BLOCK)], next_read, one_s.at[5], one_r.at[10], tm=prv)
+    rows_copy.start()
+    run_copy = send(rowrun.at[0], next_run, one_s.at[9], one_r.at[11], tm=prv)
+    run_copy.start()
+
+    fetch[1].wait()
+    fetch[2].wait()
+    spread = (
+        lax.broadcasted_iota(jnp.int32, (CAP, 128), 1) % CAP
+        == lax.broadcasted_iota(jnp.int32, (CAP, 128), 0)
+    ).astype(F32)
+    start_f = start_ref[...].astype(F32)
+    end_f = end_ref[...].astype(F32)
+    start_row = jnp.dot(jnp.broadcast_to(start_f, (8, CAP)), spread, precision=HIGH, preferred_element_type=F32)
+    end_row = jnp.dot(jnp.broadcast_to(end_f, (8, CAP)), spread, precision=HIGH, preferred_element_type=F32)
+    meta[0] = start_row
+    meta[1] = end_row
+    eye = lax.broadcasted_iota(jnp.int32, (CAP, CAP), 0) == lax.broadcasted_iota(jnp.int32, (CAP, CAP), 1)
+    inv_len = jnp.sum(jnp.where(eye, 1.0 / jnp.maximum(end_f - start_f, 1.0), 0.0), axis=1, keepdims=True)
+
+    meta_copy = send(meta, meta_prev, one_s.at[0], one_r.at[0], tm=nxt)
+    meta_copy.start()
 
     def local_scores(b, carry):
         rows = block_rows(b)
@@ -208,6 +222,34 @@
     lax.fori_loop(chip + 1, CHIPS, send_state, 0)
     lax.fori_loop(2, NB, local_scores, 0)
 
+    meta_copy.wait_recv()
+    lane = lax.broadcasted_iota(jnp.int32, (BLOCK, 128), 1)
+    frame = lax.broadcasted_iota(jnp.int32, (BLOCK, 128), 0)
+    seg_start = jnp.where(lane[0:8] < 64, meta[0], meta_prev[0])[0:1, :]
+    seg_end = jnp.where(lane[0:8] < 64, meta[1], meta_prev[1])[0:1, :]
+
+    def cover(b, carry):
+        t = (frame + (me * (NB * BLOCK) + b * BLOCK)).astype(F32)
+        inside = jnp.where(t >= seg_start, jnp.where(t < seg_end, 1.0, 0.0), 0.0)
+        mask[block_rows(b), :] = inside.astype(BF16)
+        return carry
+
+    lax.fori_loop(0, NB, cover, 0)
+
+    t = (frame + (me + 1) * (NB * BLOCK)).astype(F32)
+    inside = jnp.where(t >= seg_start, jnp.where(t < seg_end, 1.0, 0.0), 0.0)
+    spill[...] = jnp.where(lane < 64, inside, 0.0).astype(BF16)
+    rows_copy.wait_recv()
+    run_copy.wait_recv()
+    col = next_run[...].T
+    grow_next[...] = jnp.exp(
+        jnp.where(
+            lane_head < 2,
+            jnp.where(lane_head < 1, col[:, 0:1], col[:, 1:2]),
+            jnp.where(lane_head < 3, col[:, 2:3], col[:, 3:4]),
+        )
+    )
+
     fetch[7].wait()
     proj = mm(cgat[z], weight_ref[block_rows(z, 128), :])
     for d in (1, 15, 2, 14, 3, 13, 4, 12, 5, 11, 6, 10, 7, 9, 8):
@@ -228,35 +270,6 @@
 
     lax.fori_loop(1, N_TM, send_cols, 0)
 
-    meta_copy.wait_recv()
-    lane = lax.broadcasted_iota(jnp.int32, (BLOCK, 128), 1)
-    frame = lax.broadcasted_iota(jnp.int32, (BLOCK, 128), 0)
-    seg_start = jnp.where(lane[0:8] < 64, meta[0], meta_prev[0])[0:1, :]
-    seg_end = jnp.where(lane[0:8] < 64, meta[1], meta_prev[1])[0:1, :]
-
-    def cover(b, carry):
-        t = (frame + (me * (NB * BLOCK) + b * BLOCK)).astype(F32)
-        inside = jnp.where(t >= seg_start, jnp.where(t < seg_end, 1.0, 0.0), 0.0)
-        mask[block_rows(b), :] = inside.astype(BF16)
-        return carry
-
-    lax.fori_loop(0, NB, cover, 0)
-
-    def await_log(d, carry):
-        frm = (chip + d) % CHIPS
-        send(lgt.at[frm], lgt.at[frm], lg_s.at[frm], lg_r.at[frm], tm=frm * 2 + core).wait_recv()
-        return carry
-
-    lax.fori_loop(1, CHIPS, await_log, 0)
-
-    def take_state(m, acc):
-        send(tot_s, st_t.at[m], t_s.at[m], t_r.at[m], tm=m * 2 + core).wait_recv()
-        return jnp.exp(lgt[m][0:1, :]) * acc + st_t[m].astype(F32)
-
-    ent[core] = lax.fori_loop(0, chip, take_state, jnp.zeros((128, 128), F32))
-    ent_copy = send(ent.at[core], ent.at[core], one_s.at[4], one_r.at[4 + core], tm=pair)
-    ent_copy.start()
-
     hi = proj.astype(BF16)
     zst[0:32, :] = hi
     zst[32:64, :] = (proj - hi.astype(F32)).astype(BF16)
@@ -272,22 +285,48 @@
         ablk[b] = mm_tn(read_ref[rows, :], grown)
         return carry
 
-    lax.fori_loop(0, NB - 1, local_adjoint, 0)
-    z_copy.wait_recv()
-    before = zprev[...]
-    hi = before.astype(BF16)
-    zst[64:96, :] = hi
-    zst[96:128, :] = (before - hi.astype(F32)).astype(BF16)
-    lax.fori_loop(NB - 1, NB, local_adjoint, 0)
+    lax.fori_loop(0, NB, local_adjoint, 0)
+    g = mm(spill[...], zst[...]).astype(BF16).astype(F32)
+    spilt = mm_tn(next_read[...], (g * grow_next[...]).astype(BF16))
+    spill_adj[...] = spilt
     back = ablk[NB - 1]
     for b in range(NB - 2, -1, -1):
         back = jnp.exp(totx[b, 0:1, :]) * back + ablk[b]
+    back += jnp.exp(totx[0, 0:1, :] + totx[1, 0:1, :] + totx[2, 0:1, :] + totx[3, 0:1, :]) * spilt
     for half in range(2):
         cut = slice(128 * half, 128 * half + 128)
         adj[half] = back[:, cut]
         adj_b[half] = back[:, cut].astype(BF16)
     adj_copy = send(adj_b, pair_a, one_s.at[6], one_r.at[6], tm=pair)
     adj_copy.start()
+
+    def await_log(d, carry):
+        frm = (chip + d) % CHIPS
+        send(lgt.at[frm], lgt.at[frm], lg_s.at[frm], lg_r.at[frm], tm=frm * 2 + core).wait_recv()
+        return carry
+
+    lax.fori_loop(1, CHIPS, await_log, 0)
+
+    def take_state(m, acc):
+        send(tot_s, st_t.at[m], t_s.at[m], t_r.at[m], tm=m * 2 + core).wait_recv()
+        return jnp.exp(lgt[m][0:1, :]) * acc + st_t[m].astype(F32)
+
+    ent[core] = lax.fori_loop(0, chip, take_state, jnp.zeros((128, 128), F32))
+    ent_copy = send(ent.at[core], ent.at[core], one_s.at[4], one_r.at[4 + core], tm=pair)
+    ent_copy.start()
+
+    adj_copy.wait_recv()
+    mine = adj[core]
+    other = pair_a[core].astype(F32)
+    a0 = jnp.where(first, mine, other)
+    a1 = jnp.where(first, other, mine)
+    tot_a[...] = (a0 + jnp.exp(l0) * a1).astype(BF16)
+
+    def send_adjoint(to, carry):
+        send(tot_a, ad_t.at[chip], a_s.at[to], a_r.at[chip], tm=to * 2 + core).start()
+        return carry
+
+    lax.fori_loop(0, chip, send_adjoint, 0)
 
     send(ent.at[core], ent.at[1 - core], one_s.at[4], one_r.at[5 - core], tm=pair).wait_recv()
     halves = []
@@ -300,18 +339,15 @@
         if b < NB - 1:
             carry_state = jnp.exp(totx[b, 0:1, :]) * carry_state + sblk[b]
 
-    adj_copy.wait_recv()
-    mine = adj[core]
-    other = pair_a[core].astype(F32)
-    a0 = jnp.where(first, mine, other)
-    a1 = jnp.where(first, other, mine)
-    tot_a[...] = (a0 + jnp.exp(l0) * a1).astype(BF16)
-
-    def send_adjoint(to, carry):
-        send(tot_a, ad_t.at[chip], a_s.at[to], a_r.at[chip], tm=to * 2 + core).start()
-        return carry
-
-    lax.fori_loop(0, chip, send_adjoint, 0)
+    def pooled(b, acc):
+        rows = block_rows(b)
+        y = (out_acc[b] + growx[b] * mm(read_ref[rows, :], entry[b])).astype(BF16)
+        return acc + mm_tn(mask[rows, :], y)
+
+    pool = pooled(0, jnp.zeros((128, BLOCK), F32))
+    ppart[...] = pool[64:96, :]
+    p_copy = send(ppart, pprev, one_s.at[7], one_r.at[7], tm=prv)
+    p_copy.start()
 
     def hand_on(buf, mid, s, r, b):
         for k in range(4):
@@ -332,17 +368,13 @@
             send(buf.at[to], into.at[z], s.at[to], r.at[z], head=to).start()
 
     def local_cross(i, carry):
-        b = i
+        b = NB - 1 - i
         rows = block_rows(b)
         g = gy[b]
         xb = x_ref[rows, :]
         both = jnp.zeros((BLOCK, BLOCK), F32)
-        into = jnp.zeros((BLOCK, BLOCK), F32)
         for h in range(NH):
-            gh = g * hm[h]
-            both += decay[b * NH + h] * mm_nt(gh, xb)
-            into += mm_tn(scores[b * NH + h], gh)
-        in_acc[b] = into
+            both += decay[b * NH + h] * mm_nt(g * hm[h], xb)
         both = both.astype(BF16)
         part = mm(both, write_ref[rows, :]) + mm_nt(gg[b], entry[b])
         for k in range(4):
@@ -351,23 +383,18 @@
         wr_acc[b] = mm_tn(both, read_ref[rows, :])
         return carry
 
-    lax.fori_loop(0, NB, local_cross, 0)
-
-    def pooled(b, acc):
-        rows = block_rows(b)
-        y = (out_acc[b] + growx[b] * mm(read_ref[rows, :], entry[b])).astype(BF16)
-        return acc + mm_tn(mask[rows, :], y)
-
-    pool = pooled(0, jnp.zeros((128, BLOCK), F32))
-    ppart[...] = pool[64:96, :]
-    p_copy = send(ppart, pprev, one_s.at[7], one_r.at[7], tm=prv)
-    p_copy.start()
+    lax.fori_loop(0, NB - 1, local_cross, 0)
+    z_copy.wait_recv()
+    before = zprev[...]
+    hi = before.astype(BF16)
+    zst[64:96, :] = hi
+    zst[96:128, :] = (before - hi.astype(F32)).astype(BF16)
+    lax.fori_loop(NB - 1, NB, local_adjoint, 0)
+    lax.fori_loop(NB - 1, NB, local_cross, 0)
+
     pool = lax.fori_loop(1, NB, pooled, pool)
 
     send_sums(rs_r, mid_r, rr, rr_s, mid_r_s, rr_r)
-
-    p_copy.wait_recv()
-    plb[me] = ((pool[0:32, :] + pprev[...]) * inv_len).astype(BF16)
 
     def send_pool(d, carry):
         to = (me + d) % N_TM
@@ -382,13 +409,12 @@
     ext[core] = lax.fori_loop(0, CHIPS - 1 - chip, take_adjoint, jnp.zeros((128, 128), F32))
     ext_copy = send(ext.at[core], ext.at[core], one_s.at[8], one_r.at[8 + core], tm=pair)
     ext_copy.start()
-    lax.fori_loop(1, N_TM, send_pool, 0)
     send(ext.at[core], ext.at[1 - core], one_s.at[8], one_r.at[9 - core], tm=pair).wait_recv()
     halves = []
     for half in range(2):
         came = ext[half]
         halves.append(jnp.where(first, jnp.exp(log1[half]) * came + pair_a[half].astype(F32), came))
-    carry_adj = jnp.concatenate(halves, axis=1)
+    carry_adj = jnp.concatenate(halves, axis=1) + spill_adj[...]
     for b in range(NB - 1, -1, -1):
         leave[b] = carry_adj.astype(BF16)
         if b > 0:
@@ -403,16 +429,24 @@
         return carry
 
     lax.fori_loop(0, NB, late_write, 0)
+    p_copy.wait_recv()
+    plb[me] = ((pool[0:32, :] + pprev[...]) * inv_len).astype(BF16)
+    lax.fori_loop(1, N_TM, send_pool, 0)
 
     def late_inputs(b, carry):
         rows = block_rows(b)
-        gi_vm[rows, :] = (in_acc[b] + fadex[b] * mm(write_ref[rows, :], leave[b])).astype(BF16)
-        return carry
-
-    lax.fori_loop(0, NB, late_inputs, 0)
+        g = gy[b]
+        into = fadex[b] * mm(write_ref[rows, :], leave[b])
+        for h in range(NH):
+            into += mm_tn(scores[b * NH + h], g * hm[h])
+        gi_vm[rows, :] = into.astype(BF16)
+        return carry
+
+    lax.fori_loop(0, 2, late_inputs, 0)
+    send_sums(rs_w, mid_w, rw, rw_s, mid_w_s, rw_r)
+    lax.fori_loop(2, NB, late_inputs, 0)
     gi_copy = pltpu.make_async_copy(gi_vm, gi_ref, in_s.at[8])
     gi_copy.start()
-    send_sums(rs_w, mid_w, rw, rw_s, mid_w_s, rw_r)
 
     def await_pool(d, carry):
         frm = (me + d) % N_TM
@@ -422,7 +456,9 @@
 
     lax.fori_loop(1, N_TM, await_pool, 0)
     weight_grad = mm_tn(cols[...].reshape(N_TM * CAP, 128), plb[...].reshape(N_TM * CAP, BLOCK))
-    gow_ref[...] = jnp.where(first, weight_grad[0:64, :], weight_grad[64:128, :])
+    gow_vm[...] = jnp.where(first, weight_grad[0:64, :], weight_grad[64:128, :])
+    gow_copy = pltpu.make_async_copy(gow_vm, gow_ref, in_s.at[9])
+    gow_copy.start()
 
     def take(buf, into, s, r):
         def step(i, acc):
@@ -432,13 +468,16 @@
 
         return lax.fori_loop(0, N_HEAD // 2, step, buf[z].astype(F32))
 
-    gr_ref[...] = take(rs_r, rr, rr_s, rr_r)
-    gw_ref[...] = take(rs_w, rw, rw_s, rw_r)
-    gi_copy.wait()
+    gr_vm[...] = take(rs_r, rr, rr_s, rr_r)
+    gr_copy = pltpu.make_async_copy(gr_vm, gr_ref, in_s.at[10])
+    gr_copy.start()
+    gw_vm[...] = take(rs_w, rw, rw_s, rw_r)
+    gw_copy = pltpu.make_async_copy(gw_vm, gw_ref, in_s.at[11])
+    gw_copy.start()
 
     for d in range(1, N_HEAD):
         send(cgat.at[z], cgat.at[z], c_s.at[d], c_r.at[z], head=(z + d) % N_HEAD).wait_send()
-    for copy in (meta_copy, state_copy, lg_copy, z_copy, ent_copy, adj_copy, p_copy, ext_copy):
+    for copy in (meta_copy, rows_copy, run_copy, state_copy, lg_copy, z_copy, ent_copy, adj_copy, p_copy, ext_copy):
         copy.wait_send()
 
     def sent_tm(d, carry):
@@ -471,6 +510,8 @@
     lax.fori_loop(chip + 1, CHIPS, sent_state, 0)
     lax.fori_loop(0, chip, sent_adjoint, 0)
     lax.fori_loop(1, N_HEAD, sent_head, 0)
+    for copy in (gi_copy, gow_copy, gr_copy, gw_copy):
+        copy.wait()
 
 
 def write_out(*refs):
@@ -496,7 +537,7 @@
         V(caption_grad.shape, F32),
         V((1, CAP), jnp.int32),
         V((1, CAP), jnp.int32),
-        DMA((9,)),
+        DMA((12,)),
         V((N_HEAD, CAP, 128), BF16),
         V((N_TM, CAP, 128), BF16),
         V((2, 8, 128), F32),
@@ -519,7 +560,6 @@
         V((NB * NH, *tile), F32),
         V((NB * NH, *tile), BF16),
         V((NB, *tile), F32),
-        V((NB, *tile), F32),
         V((NB, BLOCK, 128), F32),
         V((NB, 128, BLOCK), BF16),
         V((NB, 128, BLOCK), BF16),
@@ -538,6 +578,11 @@
         V((128, 128), BF16),
         V(state, F32),
         V(state, F32),
+        V((BLOCK, 128), BF16),
+        V((8, BLOCK), F32),
+        V(tile, F32),
+        V((BLOCK, 128), BF16),
+        V((128, BLOCK), F32),
         V((CAP, BLOCK), F32),
         V((CAP, BLOCK), F32),
         V((N_TM, CAP, BLOCK), BF16),
@@ -548,12 +593,15 @@
         V((N_HEAD, 64, 128), BF16),
         V((N_HEAD, 64, 128), BF16),
         V(frame_inputs.shape, BF16),
+        V((64, 128), F32),
+        V((64, 128), F32),
+        V((64, BLOCK), F32),
         DMA((N_HEAD,)),
         DMA((N_HEAD,)),
         DMA((N_TM,)),
         DMA((N_TM,)),
-        DMA((10,)),
-        DMA((10,)),
+        DMA((12,)),
+        DMA((12,)),
         DMA((CHIPS,)),
         DMA((CHIPS,)),
         DMA((CHIPS,)),
@@ -579,7 +627,7 @@
             jax.ShapeDtypeStruct((64, BLOCK), F32),
         ),
         in_specs=[pl.BlockSpec(memory_space=pltpu.HBM)] * 8,
-        out_specs=(pl.BlockSpec(memory_space=pltpu.HBM), vmem, vmem, vmem),
+        out_specs=(pl.BlockSpec(memory_space=pltpu.HBM),) * 4,
         scratch_shapes=scratch,
         compiler_params=pltpu.CompilerParams(
             collective_id=0, has_side_effects=True, vmem_limit_bytes=63 * 1024 * 1024

time: 63.7 us -> 58.2 us (0.914); the launches traced: 63.6 us -> 57.2 us
  Pallas kernels: 62.9 us -> 56.6 us
    pallas_call x1, Pallas kernels: 61 us -> 54.6 us  [body(): pl.pallas_call(kernel, out_shape=(jax.ShapeDtypeStruct((frames, width), B...]
where the time goes in v3:
time: 58.2 us; the launch traced here: 57.2 us
  Pallas kernels  56.6 us (97%)
  between operations  0.64 us (1%)
    pallas_call x1, Pallas kernels, body(): pl.pallas_call(kernel, out_shape=(jax.ShapeDtypeStruct((frames, width), B...  54.6 us
    pallas_call x1, Pallas kernels, body(): pl.pallas_call(write_out, out_shape=tuple((jax.ShapeDtypeStruct(r.shape,...  1.93 us

profile of v3, /device:TPU:24, one launch (start us, length us, event | category | flops | bytes accessed | tf_op | source)
XLA Modules:
  0.0 57.2 jit_solution(10688028887356207018)
XLA Ops:
  0.6 54.6 %shard_map.111 = (bf16[1024,256]{1,0:T(8,128)(2,1)}, f32[64,128]{1,0:T(8,128)}, f32[64,128]{1,0:T(8,128)}, f32[64,256]{1,0:T(8,128)}) custom-call(bf16[1024,256]{1,0:T(8,128)(2,1)} %x_hbm.1, bf16[1024,128]{1,0:T(8,128)(2,1)} %write_hbm.1, bf16[1024,128]{1,0:T(8,128)(2,1)} %read_hbm.1, f32[4,1024]{1,0:T(4,128)} %decay_hbm.1, bf16[2048,256]{1,0:T(8,128)(2,1)} %weight_hbm.1, ...), custom_call_target="tpu_custom_call" | custom-call | tf_op jit(solution)/shard_map/pallas_call | solution.py:621
  55.3 1.9 %shard_map.112 = (bf16[1024,256]{1,0:T(8,128)(2,1)}, f32[64,128]{1,0:T(8,128)}, f32[64,128]{1,0:T(8,128)}, f32[64,256]{1,0:T(8,128)}) custom-call(bf16[1024,256]{1,0:T(8,128)(2,1)} %get-tuple-element.8.refs_0_, f32[64,128]{1,0:T(8,128)} %get-tuple-element.9.refs_1_, f32[64,128]{1,0:T(8,128)} %get-tuple-element.10.refs_2_, f32[64,256]{1,0:T(8,128)} %get-tuple-element.11.refs_3_), custom_call_target="tpu_custom_call" | custom-call | tf_op jit(solution)/shard_map/pallas_call | solution.py:639

commit v4 on v3

--- a/solution.py
+++ b/solution.py
@@ -43,7 +43,7 @@
     ld8, rowrun, growx, fadex, totx, xf, gg, gy, sblk, ablk, decay, scores,
     out_acc, wr_acc, entry, leave,
     dev, dev_b, pair_s, pair_a, adj, adj_b, lg, lg_pair, lgt, st_t, ad_t, tot_s, tot_a, ent, ext,
-    next_read, next_run, grow_next, spill, spill_adj,
+    next_read, next_run, pull, pull_next, pull_all, spill, spill_adj,
     ppart, pprev, plb, rs_r, rs_w, mid_r, mid_w, rr, rw, gi_vm, gw_vm, gr_vm, gow_vm,
     c_s, c_r, cols_s, cols_r, one_s, one_r, lg_s, lg_r, t_s, t_r, a_s, a_r, pl_s, pl_r, rr_s, rr_r, rw_s, rw_r, mid_r_s, mid_w_s,
 ):
@@ -242,13 +242,38 @@
     rows_copy.wait_recv()
     run_copy.wait_recv()
     col = next_run[...].T
-    grow_next[...] = jnp.exp(
+    growth_next = jnp.exp(
         jnp.where(
             lane_head < 2,
             jnp.where(lane_head < 1, col[:, 0:1], col[:, 1:2]),
             jnp.where(lane_head < 3, col[:, 2:3], col[:, 3:4]),
         )
     )
+
+    for h in range(NH):
+        pull[h] = jnp.zeros((128, 128), F32)
+
+    def local_pull(i, carry):
+        b = NB - 1 - i
+        rows = block_rows(b)
+        grown = growx[b]
+        total = totx[b, 0:1, :]
+        reads = read_ref[rows, :].astype(F32)
+        for h in range(NH):
+            one = slice(64 * h, 64 * h + 1)
+            scaled = (reads * grown[:, one]).astype(BF16)
+            pull[h] = jnp.exp(total[:, one]) * pull[h] + mm_tn(scaled, mask[rows, :])
+        return carry
+
+    lax.fori_loop(0, NB, local_pull, 0)
+    dev_log = totx[0, 0:1, :] + totx[1, 0:1, :] + totx[2, 0:1, :] + totx[3, 0:1, :]
+    reads = next_read[...].astype(F32)
+    for h in range(NH):
+        one = slice(64 * h, 64 * h + 1)
+        scaled = (reads * growth_next[:, one]).astype(BF16)
+        part = mm_tn(scaled, spill[...])
+        pull_next[h] = part.astype(BF16)
+        pull_all[h] = (pull[h] + jnp.exp(dev_log[:, one]) * part).astype(BF16)
 
     fetch[7].wait()
     proj = mm(cgat[z], weight_ref[block_rows(z, 128), :])
@@ -261,44 +286,34 @@
     z_copy = send(zown, zprev, one_s.at[3], one_r.at[3], tm=nxt)
     z_copy.start()
 
-    cols[me] = cgat[chip]
-
-    def send_cols(d, carry):
-        to = (me + d) % N_TM
-        send(cgat.at[to // 2], cols.at[me], cols_s.at[to], cols_r.at[me], tm=to).start()
-        return carry
-
-    lax.fori_loop(1, N_TM, send_cols, 0)
-
     hi = proj.astype(BF16)
     zst[0:32, :] = hi
     zst[32:64, :] = (proj - hi.astype(F32)).astype(BF16)
     zst[64:128, :] = jnp.zeros((64, BLOCK), BF16)
 
-    def local_adjoint(i, carry):
-        b = NB - 1 - i
-        rows = block_rows(b)
-        g = mm(mask[rows, :], zst[...]).astype(BF16)
-        gy[b] = g
-        grown = (g.astype(F32) * growx[b]).astype(BF16)
-        gg[b] = grown
-        ablk[b] = mm_tn(read_ref[rows, :], grown)
-        return carry
-
-    lax.fori_loop(0, NB, local_adjoint, 0)
-    g = mm(spill[...], zst[...]).astype(BF16).astype(F32)
-    spilt = mm_tn(next_read[...], (g * grow_next[...]).astype(BF16))
-    spill_adj[...] = spilt
-    back = ablk[NB - 1]
-    for b in range(NB - 2, -1, -1):
-        back = jnp.exp(totx[b, 0:1, :]) * back + ablk[b]
-    back += jnp.exp(totx[0, 0:1, :] + totx[1, 0:1, :] + totx[2, 0:1, :] + totx[3, 0:1, :]) * spilt
+    rows_z = [zst[...] * hm[h, 0:128, :] for h in range(NH)]
+    back = mm(pull_all[0], rows_z[0])
+    for h in range(1, NH):
+        back += mm(pull_all[h], rows_z[h])
     for half in range(2):
         cut = slice(128 * half, 128 * half + 128)
         adj[half] = back[:, cut]
         adj_b[half] = back[:, cut].astype(BF16)
     adj_copy = send(adj_b, pair_a, one_s.at[6], one_r.at[6], tm=pair)
     adj_copy.start()
+    spilt = mm(pull_next[0], rows_z[0])
+    for h in range(1, NH):
+        spilt += mm(pull_next[h], rows_z[h])
+    spill_adj[...] = spilt
+
+    cols[me] = cgat[chip]
+
+    def send_cols(d, carry):
+        to = (me + d) % N_TM
+        send(cgat.at[to // 2], cols.at[me], cols_s.at[to], cols_r.at[me], tm=to).start()
+        return carry
+
+    lax.fori_loop(1, N_TM, send_cols, 0)
 
     def await_log(d, carry):
         frm = (chip + d) % CHIPS
@@ -339,16 +354,6 @@
         if b < NB - 1:
             carry_state = jnp.exp(totx[b, 0:1, :]) * carry_state + sblk[b]
 
-    def pooled(b, acc):
-        rows = block_rows(b)
-        y = (out_acc[b] + growx[b] * mm(read_ref[rows, :], entry[b])).astype(BF16)
-        return acc + mm_tn(mask[rows, :], y)
-
-    pool = pooled(0, jnp.zeros((128, BLOCK), F32))
-    ppart[...] = pool[64:96, :]
-    p_copy = send(ppart, pprev, one_s.at[7], one_r.at[7], tm=prv)
-    p_copy.start()
-
     def hand_on(buf, mid, s, r, b):
         for k in range(4):
             to = b * 4 + k
@@ -366,6 +371,20 @@
                 send(buf.at[to], mid.at[to], s.at[to], m.at[to], head=to).wait_recv()
                 buf[to] = (buf[to].astype(F32) + mid[to].astype(F32)).astype(BF16)
             send(buf.at[to], into.at[z], s.at[to], r.at[z], head=to).start()
+
+    def local_adjoint(i, carry):
+        b = NB - 1 - i
+        rows = block_rows(b)
+        g = mm(mask[rows, :], zst[...]).astype(BF16)
+        gy[b] = g
+        grown = (g.astype(F32) * growx[b]).astype(BF16)
+        gg[b] = grown
+        return carry
+
+    def block_adjoint(i, carry):
+        b = NB - 1 - i
+        ablk[b] = mm_tn(read_ref[block_rows(b), :], gg[b])
+        return carry
 
     def local_cross(i, carry):
         b = NB - 1 - i
@@ -383,16 +402,29 @@
         wr_acc[b] = mm_tn(both, read_ref[rows, :])
         return carry
 
-    lax.fori_loop(0, NB - 1, local_cross, 0)
+    def cotangent_and_cross(i, carry):
+        return local_cross(i, local_adjoint(i, carry))
+
+    lax.fori_loop(0, NB - 1, cotangent_and_cross, 0)
     z_copy.wait_recv()
     before = zprev[...]
     hi = before.astype(BF16)
     zst[64:96, :] = hi
     zst[96:128, :] = (before - hi.astype(F32)).astype(BF16)
-    lax.fori_loop(NB - 1, NB, local_adjoint, 0)
-    lax.fori_loop(NB - 1, NB, local_cross, 0)
+    lax.fori_loop(NB - 1, NB, cotangent_and_cross, 0)
+
+    def pooled(b, acc):
+        rows = block_rows(b)
+        y = (out_acc[b] + growx[b] * mm(read_ref[rows, :], entry[b])).astype(BF16)
+        return acc + mm_tn(mask[rows, :], y)
+
+    pool = pooled(0, jnp.zeros((128, BLOCK), F32))
+    ppart[...] = pool[64:96, :]
+    p_copy = send(ppart, pprev, one_s.at[7], one_r.at[7], tm=prv)
+    p_copy.start()
 
     pool = lax.fori_loop(1, NB, pooled, pool)
+    lax.fori_loop(0, NB - 1, block_adjoint, 0)
 
     send_sums(rs_r, mid_r, rr, rr_s, mid_r_s, rr_r)
 
@@ -471,9 +503,6 @@
     gr_vm[...] = take(rs_r, rr, rr_s, rr_r)
     gr_copy = pltpu.make_async_copy(gr_vm, gr_ref, in_s.at[10])
     gr_copy.start()
-    gw_vm[...] = take(rs_w, rw, rw_s, rw_r)
-    gw_copy = pltpu.make_async_copy(gw_vm, gw_ref, in_s.at[11])
-    gw_copy.start()
 
     for d in range(1, N_HEAD):
         send(cgat.at[z], cgat.at[z], c_s.at[d], c_r.at[z], head=(z + d) % N_HEAD).wait_send()
@@ -499,26 +528,38 @@
         send(tot_a, ad_t.at[chip], a_s.at[to], a_r.at[chip], tm=to * 2 + core).wait_send()
         return carry
 
+    lax.fori_loop(1, N_TM, sent_tm, 0)
+    lax.fori_loop(1, CHIPS, sent_log, 0)
+    lax.fori_loop(chip + 1, CHIPS, sent_state, 0)
+    lax.fori_loop(0, chip, sent_adjoint, 0)
+
+    gw_vm[...] = take(rs_w, rw, rw_s, rw_r)
+    gw_copy = pltpu.make_async_copy(gw_vm, gw_ref, in_s.at[11])
+    gw_copy.start()
+
     def sent_head(d, carry):
         to = (z + d) % N_HEAD
         send(rs_r.at[to], rr.at[z], rr_s.at[to], rr_r.at[z], head=to).wait_send()
         send(rs_w.at[to], rw.at[z], rw_s.at[to], rw_r.at[z], head=to).wait_send()
         return carry
 
-    lax.fori_loop(1, N_TM, sent_tm, 0)
-    lax.fori_loop(1, CHIPS, sent_log, 0)
-    lax.fori_loop(chip + 1, CHIPS, sent_state, 0)
-    lax.fori_loop(0, chip, sent_adjoint, 0)
     lax.fori_loop(1, N_HEAD, sent_head, 0)
     for copy in (gi_copy, gow_copy, gr_copy, gw_copy):
         copy.wait()
 
 
-def write_out(*refs):
-    copies = [pltpu.make_async_copy(refs[i], refs[4 + i], refs[8].at[i]) for i in range(4)]
-    for copy in copies:
+def write_out(gi, gw, gr, gow, gi_out, gw_out, gr_out, gow_out, gi_vm, gw_vm, gr_vm, gow_vm, came, left):
+    size = gi.shape[0] // 4
+    moves = [(gi.at[pl.ds(i * size, size)], gi_vm.at[pl.ds(i * size, size)], gi_out.at[pl.ds(i * size, size)]) for i in range(4)]
+    moves += [(gw, gw_vm, gw_out), (gr, gr_vm, gr_out), (gow, gow_vm, gow_out)]
+    ins = [pltpu.make_async_copy(a, b, came.at[i]) for i, (a, b, _) in enumerate(moves)]
+    outs = [pltpu.make_async_copy(b, c, left.at[i]) for i, (_, b, c) in enumerate(moves)]
+    for copy in ins:
         copy.start()
-    for copy in copies:
+    for here, there in zip(ins, outs):
+        here.wait()
+        there.start()
+    for copy in outs:
         copy.wait()
 
 
@@ -580,7 +621,9 @@
         V(state, F32),
         V((BLOCK, 128), BF16),
         V((8, BLOCK), F32),
-        V(tile, F32),
+        V((NH, 128, 128), F32),
+        V((NH, 128, 128), BF16),
+        V((NH, 128, 128), BF16),
         V((BLOCK, 128), BF16),
         V((128, BLOCK), F32),
         V((CAP, BLOCK), F32),
@@ -617,7 +660,6 @@
         DMA((N_HEAD,)),
         DMA((N_HEAD,)),
     ]
-    vmem = pl.BlockSpec(memory_space=pltpu.VMEM)
     results = pl.pallas_call(
         kernel,
         out_shape=(
@@ -639,9 +681,9 @@
     return pl.pallas_call(
         write_out,
         out_shape=tuple(jax.ShapeDtypeStruct(r.shape, r.dtype) for r in results),
-        in_specs=[vmem] * 4,
-        out_specs=(pl.BlockSpec(memory_space=pl.ANY),) * 4,
-        scratch_shapes=[DMA((4,))],
+        in_specs=[pl.BlockSpec(memory_space=pltpu.HBM)] * 4,
+        out_specs=(pl.BlockSpec(memory_space=pltpu.HBM),) * 4,
+        scratch_shapes=[V(r.shape, r.dtype) for r in results] + [DMA((7,)), DMA((7,))],
         compiler_params=pltpu.CompilerParams(vmem_limit_bytes=62 * 1024 * 1024),
     )(*results)
 

time: 58.2 us -> 56.9 us (0.978)
  Pallas kernels: 56.6 us -> 55.5 us
    pallas_call x1, Pallas kernels: 54.6 us -> 53.6 us  [body(): pl.pallas_call(kernel, out_shape=(jax.ShapeDtypeStruct((frames, width), B...]
where the time goes in v4:
time: 56.9 us; the launch traced here: 56.1 us
  Pallas kernels  55.5 us (98%)
  between operations  0.64 us (1%)
    pallas_call x1, Pallas kernels, body(): pl.pallas_call(kernel, out_shape=(jax.ShapeDtypeStruct((frames, width), B...  53.6 us
    pallas_call x1, Pallas kernels, body(): pl.pallas_call(write_out, out_shape=tuple((jax.ShapeDtypeStruct(r.shape,...  1.91 us

profile of v4, /device:TPU:24, one launch (start us, length us, event | category | flops | bytes accessed | tf_op | source)
XLA Modules:
  0.0 56.1 jit_solution(2780479425122892756)
XLA Ops:
  0.6 53.6 %shard_map.111 = (bf16[1024,256]{1,0:T(8,128)(2,1)}, f32[64,128]{1,0:T(8,128)}, f32[64,128]{1,0:T(8,128)}, f32[64,256]{1,0:T(8,128)}) custom-call(bf16[1024,256]{1,0:T(8,128)(2,1)} %x_hbm.1, bf16[1024,128]{1,0:T(8,128)(2,1)} %write_hbm.1, bf16[1024,128]{1,0:T(8,128)(2,1)} %read_hbm.1, f32[4,1024]{1,0:T(4,128)} %decay_hbm.1, bf16[2048,256]{1,0:T(8,128)(2,1)} %weight_hbm.1, ...), custom_call_target="tpu_custom_call" | custom-call | tf_op jit(solution)/shard_map/pallas_call | solution.py:663
  54.2 1.9 %shard_map.112 = (bf16[1024,256]{1,0:T(8,128)(2,1)}, f32[64,128]{1,0:T(8,128)}, f32[64,128]{1,0:T(8,128)}, f32[64,256]{1,0:T(8,128)}) custom-call(bf16[1024,256]{1,0:T(8,128)(2,1)} %get-tuple-element.8.gi, f32[64,128]{1,0:T(8,128)} %get-tuple-element.9.gw, f32[64,128]{1,0:T(8,128)} %get-tuple-element.10.gr, f32[64,256]{1,0:T(8,128)} %get-tuple-element.11.gow), custom_call_target="tpu_custom_call" | custom-call | tf_op jit(solution)/shard_map/pallas_call | solution.py:681

commit v5 on v4

--- a/solution.py
+++ b/solution.py
@@ -301,19 +301,6 @@
         adj_b[half] = back[:, cut].astype(BF16)
     adj_copy = send(adj_b, pair_a, one_s.at[6], one_r.at[6], tm=pair)
     adj_copy.start()
-    spilt = mm(pull_next[0], rows_z[0])
-    for h in range(1, NH):
-        spilt += mm(pull_next[h], rows_z[h])
-    spill_adj[...] = spilt
-
-    cols[me] = cgat[chip]
-
-    def send_cols(d, carry):
-        to = (me + d) % N_TM
-        send(cgat.at[to // 2], cols.at[me], cols_s.at[to], cols_r.at[me], tm=to).start()
-        return carry
-
-    lax.fori_loop(1, N_TM, send_cols, 0)
 
     def await_log(d, carry):
         frm = (chip + d) % CHIPS
@@ -365,7 +352,7 @@
                 send(buf.at[to], mid.at[to], s.at[to], r.at[to], head=near).start()
 
     def send_sums(buf, mid, into, s, m, r):
-        for off in (7, 9, 5, 11, 3, 13, 1, 15):
+        for off in (9, 7, 5, 11, 3, 13, 1, 15):
             to = (z + off) % N_HEAD
             if off != 9:
                 send(buf.at[to], mid.at[to], s.at[to], m.at[to], head=to).wait_recv()
@@ -425,6 +412,20 @@
 
     pool = lax.fori_loop(1, NB, pooled, pool)
     lax.fori_loop(0, NB - 1, block_adjoint, 0)
+    spilt = mm(pull_next[0], rows_z[0])
+    for h in range(1, NH):
+        spilt += mm(pull_next[h], rows_z[h])
+    spill_adj[...] = spilt
+
+    cols[me] = cgat[chip]
+
+    def send_cols(d, carry):
+        to = (me + d) % N_TM
+        send(cgat.at[to // 2], cols.at[me], cols_s.at[to], cols_r.at[me], tm=to).start()
+        return carry
+
+    lax.fori_loop(1, N_TM, send_cols, 0)
+
 
     send_sums(rs_r, mid_r, rr, rr_s, mid_r_s, rr_r)
 
@@ -441,6 +442,9 @@
     ext[core] = lax.fori_loop(0, CHIPS - 1 - chip, take_adjoint, jnp.zeros((128, 128), F32))
     ext_copy = send(ext.at[core], ext.at[core], one_s.at[8], one_r.at[8 + core], tm=pair)
     ext_copy.start()
+    p_copy.wait_recv()
+    plb[me] = ((pool[0:32, :] + pprev[...]) * inv_len).astype(BF16)
+    lax.fori_loop(1, N_TM, send_pool, 0)
     send(ext.at[core], ext.at[1 - core], one_s.at[8], one_r.at[9 - core], tm=pair).wait_recv()
     halves = []
     for half in range(2):
@@ -461,9 +465,6 @@
         return carry
 
     lax.fori_loop(0, NB, late_write, 0)
-    p_copy.wait_recv()
-    plb[me] = ((pool[0:32, :] + pprev[...]) * inv_len).astype(BF16)
-    lax.fori_loop(1, N_TM, send_pool, 0)
 
     def late_inputs(b, carry):
         rows = block_rows(b)

time: 56.9 us -> 56 us (0.984)
  Pallas kernels: 55.5 us -> 54.9 us
    pallas_call x1, Pallas kernels: 53.6 us -> 53 us  [body(): pl.pallas_call(kernel, out_shape=(jax.ShapeDtypeStruct((frames, width), B...]
where the time goes in v5:
time: 56 us; the launch traced here: 55.5 us
  Pallas kernels  54.9 us (98%)
  between operations  0.64 us (1%)
    pallas_call x1, Pallas kernels, body(): pl.pallas_call(kernel, out_shape=(jax.ShapeDtypeStruct((frames, width), B...  53 us
    pallas_call x1, Pallas kernels, body(): pl.pallas_call(write_out, out_shape=tuple((jax.ShapeDtypeStruct(r.shape,...  1.91 us

profile of v5, /device:TPU:24, one launch (start us, length us, event | category | flops | bytes accessed | tf_op | source)
XLA Modules:
  0.0 55.5 jit_solution(617845910749986801)
XLA Ops:
  0.6 53.0 %shard_map.111 = (bf16[1024,256]{1,0:T(8,128)(2,1)}, f32[64,128]{1,0:T(8,128)}, f32[64,128]{1,0:T(8,128)}, f32[64,256]{1,0:T(8,128)}) custom-call(bf16[1024,256]{1,0:T(8,128)(2,1)} %x_hbm.1, bf16[1024,128]{1,0:T(8,128)(2,1)} %write_hbm.1, bf16[1024,128]{1,0:T(8,128)(2,1)} %read_hbm.1, f32[4,1024]{1,0:T(4,128)} %decay_hbm.1, bf16[2048,256]{1,0:T(8,128)(2,1)} %weight_hbm.1, ...), custom_call_target="tpu_custom_call" | custom-call | tf_op jit(solution)/shard_map/pallas_call | solution.py:664
  53.6 1.9 %shard_map.112 = (bf16[1024,256]{1,0:T(8,128)(2,1)}, f32[64,128]{1,0:T(8,128)}, f32[64,128]{1,0:T(8,128)}, f32[64,256]{1,0:T(8,128)}) custom-call(bf16[1024,256]{1,0:T(8,128)(2,1)} %get-tuple-element.8.gi, f32[64,128]{1,0:T(8,128)} %get-tuple-element.9.gw, f32[64,128]{1,0:T(8,128)} %get-tuple-element.10.gr, f32[64,256]{1,0:T(8,128)} %get-tuple-element.11.gow), custom_call_target="tpu_custom_call" | custom-call | tf_op jit(solution)/shard_map/pallas_call | solution.py:682

commit v6 on v5

--- a/solution.py
+++ b/solution.py
@@ -417,16 +417,6 @@
         spilt += mm(pull_next[h], rows_z[h])
     spill_adj[...] = spilt
 
-    cols[me] = cgat[chip]
-
-    def send_cols(d, carry):
-        to = (me + d) % N_TM
-        send(cgat.at[to // 2], cols.at[me], cols_s.at[to], cols_r.at[me], tm=to).start()
-        return carry
-
-    lax.fori_loop(1, N_TM, send_cols, 0)
-
-
     send_sums(rs_r, mid_r, rr, rr_s, mid_r_s, rr_r)
 
     def send_pool(d, carry):
@@ -465,6 +455,16 @@
         return carry
 
     lax.fori_loop(0, NB, late_write, 0)
+
+    cols[me] = cgat[chip]
+
+    def send_cols(d, carry):
+        to = (me + d) % N_TM
+        send(cgat.at[to // 2], cols.at[me], cols_s.at[to], cols_r.at[me], tm=to).start()
+        return carry
+
+    lax.fori_loop(1, N_TM, send_cols, 0)
+
 
     def late_inputs(b, carry):
         rows = block_rows(b)

time: 56 us -> 56.1 us (level)
  no operation moved by 1% of the time
where the time goes in v6:
time: 56.1 us; the launch traced here: 55.6 us
  Pallas kernels  55 us (98%)
  between operations  0.64 us (1%)
    pallas_call x1, Pallas kernels, body(): pl.pallas_call(kernel, out_shape=(jax.ShapeDtypeStruct((frames, width), B...  53 us
    pallas_call x1, Pallas kernels, body(): pl.pallas_call(write_out, out_shape=tuple((jax.ShapeDtypeStruct(r.shape,...  1.91 us

profile of v6, /device:TPU:24, one launch (start us, length us, event | category | flops | bytes accessed | tf_op | source)
XLA Modules:
  0.0 55.6 jit_solution(14634353654292571634)
XLA Ops:
  0.6 53.0 %shard_map.111 = (bf16[1024,256]{1,0:T(8,128)(2,1)}, f32[64,128]{1,0:T(8,128)}, f32[64,128]{1,0:T(8,128)}, f32[64,256]{1,0:T(8,128)}) custom-call(bf16[1024,256]{1,0:T(8,128)(2,1)} %x_hbm.1, bf16[1024,128]{1,0:T(8,128)(2,1)} %write_hbm.1, bf16[1024,128]{1,0:T(8,128)(2,1)} %read_hbm.1, f32[4,1024]{1,0:T(4,128)} %decay_hbm.1, bf16[2048,256]{1,0:T(8,128)(2,1)} %weight_hbm.1, ...), custom_call_target="tpu_custom_call" | custom-call | tf_op jit(solution)/shard_map/pallas_call | solution.py:664
  53.7 1.9 %shard_map.112 = (bf16[1024,256]{1,0:T(8,128)(2,1)}, f32[64,128]{1,0:T(8,128)}, f32[64,128]{1,0:T(8,128)}, f32[64,256]{1,0:T(8,128)}) custom-call(bf16[1024,256]{1,0:T(8,128)(2,1)} %get-tuple-element.8.gi, f32[64,128]{1,0:T(8,128)} %get-tuple-element.9.gw, f32[64,128]{1,0:T(8,128)} %get-tuple-element.10.gr, f32[64,256]{1,0:T(8,128)} %get-tuple-element.11.gow), custom_call_target="tpu_custom_call" | custom-call | tf_op jit(solution)/shard_map/pallas_call | solution.py:682
